TPU v7x, 256 devices: a whole 4x4x8 slice. The times are simulated.
256 devices in a mesh: lat: 32 (over y_lo, z, core), lon: 8 (over y_hi, x).
Axes of the slice: x: 4, y: 4 (y_hi: 2, y_lo: 2; y = y_hi * 2 + y_lo), z: 8, core: 2. Of those that a mesh axis runs over, the one named last changes fastest.
Arguments:
- cotangent: bfloat16 [384, 384, 1024], P(None, 'lat', 'lon'), may hold values from -6 to 6
- layer_input: bfloat16 [384, 384, 1024], P(None, 'lat', 'lon'), may hold values from -6 to 6
- filter_values: bfloat16 [3, 384, 4, 17], replicated, may hold values from -4 to 4
- weights: bfloat16 [3, 384, 384], replicated, may hold values from -0.1875 to 0.1875
- row_offset: int32 [384], replicated, may hold values from -3 to 0, as said below
- reach: int32 [384], replicated, may hold values from 1 to 9, as said below
Outputs:
- input_grad: bfloat16 [384, 384, 1024], P(None, 'lat', 'lon')
- weight_grad: float32 [3, 384, 384], replicated
Inputs may be any that keep to these rules, and one draw needn't show every extreme that they name: The support rows of output latitude o are o + row_offset[o] to o + row_offset[o] + 3. Taps d with |d| < reach[o] are used.
All inputs are finite; a program needn't handle non-finite values.
Results may differ from a plain program's by a relative error of at most 0.0049.
Values may be sent and summed in bfloat16 or wider, within the bound.
A program may use at most 128 MiB of HBM per device.

v0:
```python
import jax
import jax.numpy as jnp
from jax import lax
from jax.sharding import PartitionSpec as P


def with_halo(x, sides, width):
    for axis, dim in sides:
        devices, length = (lax.axis_size(axis), x.shape[dim])
        up = [(i, (i + 1) % devices) for i in range(devices - 1)]
        down = [(j, i) for i, j in up]
        last = lax.slice_in_dim(x, length - width, length, axis=dim)
        first = lax.slice_in_dim(x, 0, width, axis=dim)
        before = lax.ppermute(last, axis, up)
        after = lax.ppermute(first, axis, down)
        x = jnp.concatenate([before, x, after], axis=dim)
    return x


def on_device(cotangent, layer_input, filter_values, weights, row_offset, reach):
    feature_channels, rows, cols = cotangent.shape
    kernels, nlat, span, taps = filter_values.shape
    reach_q = (taps - 1) // 2
    rim = span - 1
    tall = rows + 2 * rim
    first_row = lax.axis_index("lat") * rows
    padded = with_halo(cotangent, (("lat", 1),), rim)
    source = first_row - rim + jnp.arange(tall, dtype=jnp.int32)
    inside = (source >= 0) & (source < nlat)
    safe = jnp.clip(source, 0, nlat - 1)
    offsets = jnp.take(row_offset, safe)
    tap_reach_list = jnp.where(inside, jnp.take(reach, safe), 0)
    psi_rows = jnp.take(filter_values, safe, axis=1).astype(jnp.float32)
    tap_ids = jnp.arange(taps, dtype=jnp.int32) - reach_q
    live = (jnp.abs(tap_ids)[None, :] < tap_reach_list[:, None]).astype(jnp.float32)
    level = (
        jnp.arange(rows, dtype=jnp.int32)[:, None]
        - jnp.arange(tall, dtype=jnp.int32)[None, :]
        + rim
        - offsets[None, :]
    )
    pick = (level[:, :, None] == jnp.arange(span, dtype=jnp.int32)[None, None, :]).astype(
        jnp.float32
    )
    mixing = jnp.einsum("ios,kost->ktio", pick, psi_rows * live[None, :, None, :]).astype(
        jnp.bfloat16
    )
    widest = jnp.max(tap_reach_list)
    lower = reach_q - widest + 1
    upper = reach_q + widest
    moved = lax.all_to_all(padded, "lon", split_axis=0, concat_axis=2, tiled=True)
    wide = jnp.concatenate([moved[:, :, -reach_q:], moved, moved[:, :, :reach_q]], axis=2)
    out_cols = wide.shape[2] - 2 * reach_q
    local_channels = wide.shape[0]

    def add_tap(tap, total):
        shifted = lax.dynamic_slice_in_dim(wide, 2 * reach_q - tap, out_cols, 2)
        mix_tap = lax.dynamic_index_in_dim(mixing, tap, 1, keepdims=False)
        return total + jnp.einsum(
            "kio,col->kcil", mix_tap, shifted, preferred_element_type=jnp.float32
        )

    start = jnp.zeros((kernels, local_channels, rows, out_cols), jnp.float32)
    tap_spread_width = lax.fori_loop(lower, upper, add_tap, start).astype(jnp.bfloat16)
    tap_spread_width = lax.all_to_all(
        tap_spread_width, "lon", split_axis=3, concat_axis=1, tiled=True
    )
    input_grad = lax.dot_general(
        weights, tap_spread_width, (((0, 1), (0, 1)), ((), ())), preferred_element_type=jnp.float32
    )
    partial_grad = lax.dot_general(
        tap_spread_width,
        layer_input,
        (((2, 3), (1, 2)), ((), ())),
        preferred_element_type=jnp.float32,
    )
    total_grad = lax.psum(partial_grad, ("lat", "lon"))
    longitude_count_full = cols * lax.axis_size("lon")
    weight_grad = total_grad / jnp.sqrt(jnp.float32(nlat * longitude_count_full))
    return (input_grad.astype(jnp.bfloat16), weight_grad)


def solution(mesh):
    return jax.shard_map(
        on_device,
        mesh=mesh,
        in_specs=(P(None, "lat", "lon"), P(None, "lat", "lon"), P(), P(), P(), P()),
        out_specs=(P(None, "lat", "lon"), P()),
        check_vma=False,
    )
```

profile of v0, /device:TPU:1, one launch (start us, length us, event | category | flops | bytes accessed | tf_op | source)
XLA Modules:
  0.0 650.3 jit_solution(12407384555351623323)
XLA Ops:
  9.1 4.9 collective-permute-start
  25.2 6.8 %all-to-all-start = ((bf16[384,18,128]{2,1,0:T(8,128)(2,1)}), bf16[384,18,128]{2,1,0:T(8,128)(2,1)S(1)}, u32[]{:S(2)}, u32[]{:S(2)}) async-start(bf16[384,18,128]{2,1,0:T(8,128)(2,1)} %pad_maximum_fusion), calls=%async_computation | async-start | bytes 4718592 | tf_op jit(solution)/shard_map/all_to_all | solution.py:51
  46.0 13.8 %all-to-all-done = bf16[384,18,128]{2,1,0:T(8,128)(2,1)S(1)} async-done(((bf16[384,18,128]{2,1,0:T(8,128)(2,1)}), bf16[384,18,128]{2,1,0:T(8,128)(2,1)S(1)}, u32[]{:S(2)}, u32[]{:S(2)}) %all-to-all-start) | async-done | bytes 1769504 | tf_op jit(solution)/shard_map/all_to_all | solution.py:51
  66.1 4.4 concatenate.7
  70.5 4.8 broadcast_in_dim.17
  75.4 183.5 %while.12 = (s32[]{:T(128)}, f32[3,48,12,1024]{3,2,0,1:T(8,128)}, s32[]{:T(128)}, bf16[48,18,1040]{2,0,1:T(8,128)(2,1)S(1)}, bf16[3,17,12,18]{3,2,0,1:T(8,128)(2...) while((s32[]{:T(128)}, f32[3,48,12,1024]{3,2,0,1:T(8,128)}, s32[]{:T(128)}, ...), condition=%wide.region_2.4_spmd, body=%wide.region_1.3_spmd.sunk | while | flops 65470472 | bytes 21835972 | solution.py:64
  76.2 10.0 %bitcast_add_fusion.2 = f32[3,48,12,1024]{3,2,0,1:T(8,128)} fusion(f32[3,48,12,1024]{3,2,0,1:T(8,128)} %get-tuple-element.167, bf16[48,18,1024]{2,0,1:T(8,128)(2,1)S(1)} %constant_dynamic-slice_fusion.2, bf16[3,17,12,18]{3,2,0,1:T(8,128)(2,1)} %get-tuple-element.180, s32[]{:T(128)S(6)} %select_n.77), kind=kOutput, calls=%fused_computation.3.clone.1 | convolution fusion | flops 65470464 | bytes 18296836 | tf_op jit(solution)/shard_map/while/body/kio,col->kcil/dot_general | solution.py:59
  87.0 10.0 %bitcast_add_fusion.2 = f32[3,48,12,1024]{3,2,0,1:T(8,128)} fusion(f32[3,48,12,1024]{3,2,0,1:T(8,128)} %get-tuple-element.167, bf16[48,18,1024]{2,0,1:T(8,128)(2,1)S(1)} %constant_dynamic-slice_fusion.2, bf16[3,17,12,18]{3,2,0,1:T(8,128)(2,1)} %get-tuple-element.180, s32[]{:T(128)S(6)} %select_n.77), kind=kOutput, calls=%fused_computation.3.clone.1 | convolution fusion | flops 65470464 | bytes 18296836 | tf_op jit(solution)/shard_map/while/body/kio,col->kcil/dot_general | solution.py:59
  97.8 10.0 %bitcast_add_fusion.2 = f32[3,48,12,1024]{3,2,0,1:T(8,128)} fusion(f32[3,48,12,1024]{3,2,0,1:T(8,128)} %get-tuple-element.167, bf16[48,18,1024]{2,0,1:T(8,128)(2,1)S(1)} %constant_dynamic-slice_fusion.2, bf16[3,17,12,18]{3,2,0,1:T(8,128)(2,1)} %get-tuple-element.180, s32[]{:T(128)S(6)} %select_n.77), kind=kOutput, calls=%fused_computation.3.clone.1 | convolution fusion | flops 65470464 | bytes 18296836 | tf_op jit(solution)/shard_map/while/body/kio,col->kcil/dot_general | solution.py:59
  108.6 10.0 %bitcast_add_fusion.2 = f32[3,48,12,1024]{3,2,0,1:T(8,128)} fusion(f32[3,48,12,1024]{3,2,0,1:T(8,128)} %get-tuple-element.167, bf16[48,18,1024]{2,0,1:T(8,128)(2,1)S(1)} %constant_dynamic-slice_fusion.2, bf16[3,17,12,18]{3,2,0,1:T(8,128)(2,1)} %get-tuple-element.180, s32[]{:T(128)S(6)} %select_n.77), kind=kOutput, calls=%fused_computation.3.clone.1 | convolution fusion | flops 65470464 | bytes 18296836 | tf_op jit(solution)/shard_map/while/body/kio,col->kcil/dot_general | solution.py:59
  119.4 10.0 %bitcast_add_fusion.2 = f32[3,48,12,1024]{3,2,0,1:T(8,128)} fusion(f32[3,48,12,1024]{3,2,0,1:T(8,128)} %get-tuple-element.167, bf16[48,18,1024]{2,0,1:T(8,128)(2,1)S(1)} %constant_dynamic-slice_fusion.2, bf16[3,17,12,18]{3,2,0,1:T(8,128)(2,1)} %get-tuple-element.180, s32[]{:T(128)S(6)} %select_n.77), kind=kOutput, calls=%fused_computation.3.clone.1 | convolution fusion | flops 65470464 | bytes 18296836 | tf_op jit(solution)/shard_map/while/body/kio,col->kcil/dot_general | solution.py:59
  130.2 10.0 %bitcast_add_fusion.2 = f32[3,48,12,1024]{3,2,0,1:T(8,128)} fusion(f32[3,48,12,1024]{3,2,0,1:T(8,128)} %get-tuple-element.167, bf16[48,18,1024]{2,0,1:T(8,128)(2,1)S(1)} %constant_dynamic-slice_fusion.2, bf16[3,17,12,18]{3,2,0,1:T(8,128)(2,1)} %get-tuple-element.180, s32[]{:T(128)S(6)} %select_n.77), kind=kOutput, calls=%fused_computation.3.clone.1 | convolution fusion | flops 65470464 | bytes 18296836 | tf_op jit(solution)/shard_map/while/body/kio,col->kcil/dot_general | solution.py:59
  140.9 10.0 %bitcast_add_fusion.2 = f32[3,48,12,1024]{3,2,0,1:T(8,128)} fusion(f32[3,48,12,1024]{3,2,0,1:T(8,128)} %get-tuple-element.167, bf16[48,18,1024]{2,0,1:T(8,128)(2,1)S(1)} %constant_dynamic-slice_fusion.2, bf16[3,17,12,18]{3,2,0,1:T(8,128)(2,1)} %get-tuple-element.180, s32[]{:T(128)S(6)} %select_n.77), kind=kOutput, calls=%fused_computation.3.clone.1 | convolution fusion | flops 65470464 | bytes 18296836 | tf_op jit(solution)/shard_map/while/body/kio,col->kcil/dot_general | solution.py:59
  151.7 10.0 %bitcast_add_fusion.2 = f32[3,48,12,1024]{3,2,0,1:T(8,128)} fusion(f32[3,48,12,1024]{3,2,0,1:T(8,128)} %get-tuple-element.167, bf16[48,18,1024]{2,0,1:T(8,128)(2,1)S(1)} %constant_dynamic-slice_fusion.2, bf16[3,17,12,18]{3,2,0,1:T(8,128)(2,1)} %get-tuple-element.180, s32[]{:T(128)S(6)} %select_n.77), kind=kOutput, calls=%fused_computation.3.clone.1 | convolution fusion | flops 65470464 | bytes 18296836 | tf_op jit(solution)/shard_map/while/body/kio,col->kcil/dot_general | solution.py:59
  162.5 10.0 %bitcast_add_fusion.2 = f32[3,48,12,1024]{3,2,0,1:T(8,128)} fusion(f32[3,48,12,1024]{3,2,0,1:T(8,128)} %get-tuple-element.167, bf16[48,18,1024]{2,0,1:T(8,128)(2,1)S(1)} %constant_dynamic-slice_fusion.2, bf16[3,17,12,18]{3,2,0,1:T(8,128)(2,1)} %get-tuple-element.180, s32[]{:T(128)S(6)} %select_n.77), kind=kOutput, calls=%fused_computation.3.clone.1 | convolution fusion | flops 65470464 | bytes 18296836 | tf_op jit(solution)/shard_map/while/body/kio,col->kcil/dot_general | solution.py:59
  173.3 10.0 %bitcast_add_fusion.2 = f32[3,48,12,1024]{3,2,0,1:T(8,128)} fusion(f32[3,48,12,1024]{3,2,0,1:T(8,128)} %get-tuple-element.167, bf16[48,18,1024]{2,0,1:T(8,128)(2,1)S(1)} %constant_dynamic-slice_fusion.2, bf16[3,17,12,18]{3,2,0,1:T(8,128)(2,1)} %get-tuple-element.180, s32[]{:T(128)S(6)} %select_n.77), kind=kOutput, calls=%fused_computation.3.clone.1 | convolution fusion | flops 65470464 | bytes 18296836 | tf_op jit(solution)/shard_map/while/body/kio,col->kcil/dot_general | solution.py:59
  184.1 10.0 %bitcast_add_fusion.2 = f32[3,48,12,1024]{3,2,0,1:T(8,128)} fusion(f32[3,48,12,1024]{3,2,0,1:T(8,128)} %get-tuple-element.167, bf16[48,18,1024]{2,0,1:T(8,128)(2,1)S(1)} %constant_dynamic-slice_fusion.2, bf16[3,17,12,18]{3,2,0,1:T(8,128)(2,1)} %get-tuple-element.180, s32[]{:T(128)S(6)} %select_n.77), kind=kOutput, calls=%fused_computation.3.clone.1 | convolution fusion | flops 65470464 | bytes 18296836 | tf_op jit(solution)/shard_map/while/body/kio,col->kcil/dot_general | solution.py:59
  194.9 10.0 %bitcast_add_fusion.2 = f32[3,48,12,1024]{3,2,0,1:T(8,128)} fusion(f32[3,48,12,1024]{3,2,0,1:T(8,128)} %get-tuple-element.167, bf16[48,18,1024]{2,0,1:T(8,128)(2,1)S(1)} %constant_dynamic-slice_fusion.2, bf16[3,17,12,18]{3,2,0,1:T(8,128)(2,1)} %get-tuple-element.180, s32[]{:T(128)S(6)} %select_n.77), kind=kOutput, calls=%fused_computation.3.clone.1 | convolution fusion | flops 65470464 | bytes 18296836 | tf_op jit(solution)/shard_map/while/body/kio,col->kcil/dot_general | solution.py:59
  205.7 10.0 %bitcast_add_fusion.2 = f32[3,48,12,1024]{3,2,0,1:T(8,128)} fusion(f32[3,48,12,1024]{3,2,0,1:T(8,128)} %get-tuple-element.167, bf16[48,18,1024]{2,0,1:T(8,128)(2,1)S(1)} %constant_dynamic-slice_fusion.2, bf16[3,17,12,18]{3,2,0,1:T(8,128)(2,1)} %get-tuple-element.180, s32[]{:T(128)S(6)} %select_n.77), kind=kOutput, calls=%fused_computation.3.clone.1 | convolution fusion | flops 65470464 | bytes 18296836 | tf_op jit(solution)/shard_map/while/body/kio,col->kcil/dot_general | solution.py:59
  216.5 10.0 %bitcast_add_fusion.2 = f32[3,48,12,1024]{3,2,0,1:T(8,128)} fusion(f32[3,48,12,1024]{3,2,0,1:T(8,128)} %get-tuple-element.167, bf16[48,18,1024]{2,0,1:T(8,128)(2,1)S(1)} %constant_dynamic-slice_fusion.2, bf16[3,17,12,18]{3,2,0,1:T(8,128)(2,1)} %get-tuple-element.180, s32[]{:T(128)S(6)} %select_n.77), kind=kOutput, calls=%fused_computation.3.clone.1 | convolution fusion | flops 65470464 | bytes 18296836 | tf_op jit(solution)/shard_map/while/body/kio,col->kcil/dot_general | solution.py:59
  227.3 10.0 %bitcast_add_fusion.2 = f32[3,48,12,1024]{3,2,0,1:T(8,128)} fusion(f32[3,48,12,1024]{3,2,0,1:T(8,128)} %get-tuple-element.167, bf16[48,18,1024]{2,0,1:T(8,128)(2,1)S(1)} %constant_dynamic-slice_fusion.2, bf16[3,17,12,18]{3,2,0,1:T(8,128)(2,1)} %get-tuple-element.180, s32[]{:T(128)S(6)} %select_n.77), kind=kOutput, calls=%fused_computation.3.clone.1 | convolution fusion | flops 65470464 | bytes 18296836 | tf_op jit(solution)/shard_map/while/body/kio,col->kcil/dot_general | solution.py:59
  238.1 10.0 %bitcast_add_fusion.2 = f32[3,48,12,1024]{3,2,0,1:T(8,128)} fusion(f32[3,48,12,1024]{3,2,0,1:T(8,128)} %get-tuple-element.167, bf16[48,18,1024]{2,0,1:T(8,128)(2,1)S(1)} %constant_dynamic-slice_fusion.2, bf16[3,17,12,18]{3,2,0,1:T(8,128)(2,1)} %get-tuple-element.180, s32[]{:T(128)S(6)} %select_n.77), kind=kOutput, calls=%fused_computation.3.clone.1 | convolution fusion | flops 65470464 | bytes 18296836 | tf_op jit(solution)/shard_map/while/body/kio,col->kcil/dot_general | solution.py:59
  248.9 10.0 %bitcast_add_fusion.2 = f32[3,48,12,1024]{3,2,0,1:T(8,128)} fusion(f32[3,48,12,1024]{3,2,0,1:T(8,128)} %get-tuple-element.167, bf16[48,18,1024]{2,0,1:T(8,128)(2,1)S(1)} %constant_dynamic-slice_fusion.2, bf16[3,17,12,18]{3,2,0,1:T(8,128)(2,1)} %get-tuple-element.180, s32[]{:T(128)S(6)} %select_n.77), kind=kOutput, calls=%fused_computation.3.clone.1 | convolution fusion | flops 65470464 | bytes 18296836 | tf_op jit(solution)/shard_map/while/body/kio,col->kcil/dot_general | solution.py:59
  258.8 9.2 %copy.71 = bf16[3,48,12,1024]{3,1,2,0:T(8,128)(2,1)} copy(f32[3,48,12,1024]{3,2,0,1:T(8,128)} %get-tuple-element.71) | data formatting | bytes 10616832 | tf_op jit(solution)/shard_map/while | solution.py:64
  268.0 14.4 %copy.54 = bf16[3,48,12,1024]{1,2,0,3:T(8,128)(2,1)} copy(bf16[3,48,12,1024]{3,1,2,0:T(8,128)(2,1)} %copy.71) | data formatting | bytes 7077888 | tf_op jit(solution)/shard_map/convert_element_type | solution.py:64
  282.5 16.4 %reshape.127 = bf16[8,2,110592]{2,1,0:T(2,128)(2,1)} reshape(bf16[1024,3,12,48]{3,2,1,0:T(8,128)(2,1)} %bitcast.63) | data formatting | bytes 7077888
  298.9 48.2 %all_to_all.36 = bf16[8,2,110592]{2,1,0:T(2,128)(2,1)} all-to-all(bf16[8,2,110592]{2,1,0:T(2,128)(2,1)} %reshape.127), channel_id=1, replica_groups=mesh['lat'=32,'lon'=8] {'lon'}, dimensions={0} | all-to-all | bytes 7077888 | tf_op jit(solution)/shard_map/all_to_all | solution.py:65
  347.1 17.7 %reshape.128 = bf16[1024,3,12,48]{3,2,1,0:T(8,128)(2,1)} reshape(bf16[8,2,110592]{2,1,0:T(2,128)(2,1)} %all_to_all.36) | data formatting | bytes 7077888
  364.9 13.7 %copy.56 = bf16[3,8,48,12,128]{4,2,1,3,0:T(8,128)(2,1)} copy(bf16[3,8,48,12,128]{2,3,0,4,1:T(8,128)(2,1)} %bitcast.64) | data formatting | bytes 7077888 | tf_op jit(solution)/shard_map/all_to_all | solution.py:65
  378.6 5.3 convolution_bitcast_fusion
  383.9 4.2 fusion.3
  389.5 251.1 %all-reduce.2.cloned.1.call-done = f32[3,384,384]{2,1,0:T(8,128)} async-done(((f32[3,384,384]{2,1,0:T(8,128)}), f32[3,384,384]{2,1,0:T(8,128)}) %all-reduce.2.cloned.1.call-update) | async-done | bytes 1769488 | tf_op jit(solution)/shard_map/psum | solution.py:77
  (57 shorter events, 50.0 us)
Async XLA Ops:
  7.2 371.4 %copy-start = (bf16[384,12,128]{2,0,1:T(8,128)(2,1)S(1)}, bf16[384,12,128]{2,0,1:T(8,128)(2,1)}, u32[]{:S(2)}) copy-start(bf16[384,12,128]{2,0,1:T(8,128)(2,1)} %param.11) | copy-start | bytes 3538948
  9.1 9.2 %collective-permute-start = (bf16[384,3,128]{2,0,1:T(8,128)(2,1)}, bf16[384,3,128]{2,0,1:T(8,128)(2,1)}, u32[]{:S(2)}, u32[]{:S(2)}) collective-permute-start(bf16[384,3,128]{2,0,1:T(8,128)(2,1)} %get-tuple-element.121), channel_id=1, source_target_pairs={{0,8},{8,16},{16,24},{24,32},{32,40},{40,48},{48,56},{56,64},{64,7... | collective-permute-start | bytes 884744 | tf_op jit(solution)/shard_map/ppermute | solution.py:14
  14.0 8.0 %collective-permute-start.1 = (bf16[384,3,128]{2,0,1:T(8,128)(2,1)S(1)}, bf16[384,3,128]{2,0,1:T(8,128)(2,1)S(1)}, u32[]{:S(2)}, u32[]{:S(2)}) collective-permute-start(bf16[384,3,128]{2,0,1:T(8,128)(2,1)S(1)} %get-tuple-element.122), channel_id=1, source_target_pairs={{8,0},{16,8},{24,16},{32,24},{40,32},{48,40},{56,48},{64,56},{72,6... | collective-permute-start | bytes 884744 | tf_op jit(solution)/shard_map/ppermute | solution.py:15
  25.2 6.9 %copy-start.1 = (s32[384]{0:T(512)S(1)}, s32[384]{0:T(512)}, u32[]{:S(2)}) copy-start(s32[384]{0:T(512)} %param.14) | copy-start | bytes 4612
  25.2 7.6 %copy-start.2 = (s32[384]{0:T(512)S(1)}, s32[384]{0:T(512)}, u32[]{:S(2)}) copy-start(s32[384]{0:T(512)} %param.15) | copy-start | bytes 4612
  25.2 34.6 %all-to-all-start = ((bf16[384,18,128]{2,1,0:T(8,128)(2,1)}), bf16[384,18,128]{2,1,0:T(8,128)(2,1)S(1)}, u32[]{:S(2)}, u32[]{:S(2)}) async-start(bf16[384,18,128]{2,1,0:T(8,128)(2,1)} %pad_maximum_fusion), calls=%async_computation | async-start | bytes 4718592 | tf_op jit(solution)/shard_map/all_to_all | solution.py:51
  32.0 608.6 %all-reduce.2.cloned.1.call-start = ((), (), s32[]{:S(2)}) async-start(), calls=%async_computation.2 | async-start | bytes 3538944 | tf_op jit(solution)/shard_map/psum | solution.py:77
  64.8 1.3 copy-start.3
  378.6 5.3 copy-start.4
Sparse Core Ops, SparseCore 0:
  384.0 256.5 all-reduce.1
where the time goes:
time: 653 us; the launch traced here: 650 us
  waiting for transfers between devices  267 us (41%)
  matrix products  181 us (28%)
  local copies, waits for them, and re-layouts  117 us (18%)
  blocking collectives  48.2 us (7%)
  between operations  15.5 us (2%)
  starting transfers between devices  13.9 us (2%)
  other arithmetic  7.17 us (1%)
    psum x1, waiting for transfers between devices, on_device(): total_grad = lax.psum(partial_grad, ('lat', 'lon'))  251 us
    dot_general x17, matrix products, add_tap(): jnp.einsum('kio,col->kcil', mix_tap, shifted, preferred_element_type=jnp....  170 us
    all_to_all x1, blocking collectives, on_device(): lax.all_to_all(tap_spread_width, 'lon', split_axis=3, concat_axis=1, tile...  48.2 us
    unnamed x15, local copies, waits for them, and re-layouts  41 us
    convert_element_type x1, local copies, waits for them, and re-layouts, on_device(): lax.fori_loop(lower, upper, add_tap, start).astype(jnp.bfloat16)  14.4 us
    all_to_all x1, waiting for transfers between devices, on_device(): lax.all_to_all(padded, 'lon', split_axis=0, concat_axis=2, tiled=True)  13.8 us
    all_to_all x1, local copies, waits for them, and re-layouts, on_device(): lax.all_to_all(tap_spread_width, 'lon', split_axis=3, concat_axis=1, tile...  13.7 us
    dynamic_slice x17, local copies, waits for them, and re-layouts, add_tap(): shifted = lax.dynamic_slice_in_dim(wide, 2 * reach_q - tap, out_cols, 2)  13.6 us
  transfers between devices with their start and end apart: 4, of which 3 were waited for; matrix products, arithmetic and copies ran while one was open for 3% of the time, Pallas kernels for 0%

commit v1 on v0

v1 whole, which is shorter than its diff:
```python
import functools

import jax
import jax.numpy as jnp
from jax import lax
from jax.experimental import pallas as pl
from jax.experimental.pallas import tpu as pltpu
from jax.sharding import PartitionSpec as P

MESH = pl.DeviceIdType.MESH
F32 = jnp.float32
BF16 = jnp.bfloat16


def iota(shape, dim):
    return lax.broadcasted_iota(jnp.int32, shape, dim)


def ceil_to(n, m):
    return -(-n // m) * m


class Plan:
    def __init__(self, lat, lon, channels, rows, cols, nlat, kernels, span, taps):
        self.lat, self.lon = lat, lon
        self.c, self.rows, self.cols = channels, rows, cols
        self.nlat, self.k, self.span, self.taps = nlat, kernels, span, taps
        self.q = (taps - 1) // 2
        self.rim = span - 1
        self.tall = rows + 2 * self.rim
        self.near = 2 * span - 1
        self.pairs = rows // 2
        self.z = lat // 4
        self.xy = 2 * lon
        self.mix = kernels * channels
        self.chunk = self.mix // 6
        self.blocks = channels // 128
        self.part = self.chunk * self.blocks
        self.half = 3 * self.part
        self.piece = ceil_to(-(-self.half // self.xy), 16)
        self.sub = ceil_to(-(-self.piece // self.z), 16)
        self.window = self.near + 1
        self.band = self.window * cols
        self.deep = self.band + self.window * 16


def remote(src, dst, sems, n, device):
    return pltpu.make_async_remote_copy(
        src_ref=src,
        dst_ref=dst,
        send_sem=sems[0].at[n],
        recv_sem=sems[1].at[n],
        device_id=device,
        device_id_type=MESH,
    )


def kernel(
    g,
    cot,
    xin,
    w_in,
    fv,
    ro,
    reach,
    out,
    gathered,
    cot_s,
    x_s,
    xt,
    w_s,
    wt,
    taps_s,
    toep,
    sp,
    pack_l,
    pack_r,
    left,
    right,
    rim_s,
    grad,
    core_in,
    grad16,
    xy_in,
    own,
    z_in,
    sub16,
    own16,
    out_s,
    local_sem,
    halo_send,
    halo_recv,
    core_send,
    core_recv,
    xy_send,
    xy_recv,
    z_send,
    z_recv,
    zg_send,
    zg_recv,
    xyg_send,
    xyg_recv,
):
    lat = lax.axis_index("lat")
    lon = lax.axis_index("lon")
    core = lax.rem(lat, 2)
    zi = lax.rem(lat // 2, g.z)
    ylo = lat // (2 * g.z)
    me_xy = ylo * g.lon + lon
    up, down = lax.rem(lat + 1, g.lat), lax.rem(lat + g.lat - 1, g.lat)
    east, west = lax.rem(lon + 1, g.lon), lax.rem(lon + g.lon - 1, g.lon)
    sibling = (lat + 1 - 2 * core, lon)

    def xy_peer(d):
        peer = lax.rem(me_xy + d, g.xy)
        return peer, ((peer // g.lon) * (2 * g.z) + lax.rem(lat, 2 * g.z), lax.rem(peer, g.lon))

    def z_peer(d):
        peer = lax.rem(zi + d, g.z)
        return peer, (ylo * 2 * g.z + peer * 2 + core, lon)

    halo = [
        (up, lon),
        (down, lon),
        (lat, east),
        (lat, west),
        (up, east),
        (up, west),
        (down, east),
        (down, west),
    ]
    partners = halo + [sibling]
    partners += [xy_peer(d)[1] for d in range(1, g.xy)]
    partners += [z_peer(d)[1] for d in range(1, g.z)]

    barrier = pltpu.get_barrier_semaphore()
    for peer in partners:
        pl.semaphore_signal(barrier, inc=1, device_id=peer, device_id_type=MESH)

    load_cot = pltpu.make_async_copy(cot, cot_s.at[pl.ds(g.rim, g.rows)], local_sem.at[0])
    load_x = pltpu.make_async_copy(xin, x_s, local_sem.at[1])
    load_w = pltpu.make_async_copy(w_in, w_s, local_sem.at[2])
    load_cot.start()
    load_x.start()
    load_w.start()
    load_cot.wait()

    pick = iota((16, g.cols), 0)
    lane = iota((16, g.cols), 1)
    pick = (lane == jnp.where(pick < 8, pick + (g.cols - 8), pick - 8)).astype(F32).astype(BF16)
    for o in range(0, g.rows, 2):
        edge = [
            lax.dot_general(
                pick, cot_s[g.rim + o + n], (((1,), (1,)), ((), ())), preferred_element_type=F32
            )
            for n in range(2)
        ]
        pack_r[8 * o : 8 * o + 16, :] = jnp.concatenate([edge[0][:8], edge[1][:8]], 0).astype(BF16)
        pack_l[8 * o : 8 * o + 16, :] = jnp.concatenate([edge[0][8:], edge[1][8:]], 0).astype(BF16)

    pl.semaphore_wait(barrier, len(partners))

    sems = (halo_send, halo_recv)
    n_own = 8 * g.rows
    last = n_own - 32
    rim, tall, rows = g.rim, g.tall, g.rows
    sends = [
        remote(cot.at[pl.ds(rows - rim, rim)], cot_s.at[pl.ds(0, rim)], sems, 0, halo[0]),
        remote(cot.at[pl.ds(0, rim)], cot_s.at[pl.ds(tall - rim, rim)], sems, 1, halo[1]),
        remote(pack_r, left.at[pl.ds(32, n_own)], sems, 2, halo[2]),
        remote(pack_l, right.at[pl.ds(32, n_own)], sems, 3, halo[3]),
        remote(pack_r.at[pl.ds(last, 32)], left.at[pl.ds(0, 32)], sems, 4, halo[4]),
        remote(pack_l.at[pl.ds(last, 32)], right.at[pl.ds(0, 32)], sems, 5, halo[5]),
        remote(pack_r.at[pl.ds(0, 32)], left.at[pl.ds(32 + n_own, 32)], sems, 6, halo[6]),
        remote(pack_l.at[pl.ds(0, 32)], right.at[pl.ds(32 + n_own, 32)], sems, 7, halo[7]),
    ]
    for copy in sends:
        copy.start()

    source = iota((32, g.nlat), 1)
    slot = iota((32, g.nlat), 0)
    here = (source == lat * rows - rim + slot) & (slot < tall)
    moved = lax.dot_general(
        here.astype(F32).astype(BF16), fv[...], (((1,), (1,)), ((), ())), preferred_element_type=F32
    )
    first = jnp.sum(jnp.where(here, ro[...].astype(F32), 0.0), axis=1, keepdims=True).astype(jnp.int32)
    reached = jnp.sum(jnp.where(here, reach[...].astype(F32), 0.0), axis=1, keepdims=True)
    reached = reached.astype(jnp.int32)
    column = iota((32, 256), 1)
    level = column & 3
    order = column >> 2
    tap = order
    for n in range(1, g.k):
        tap = tap - jnp.where(order >= n * g.taps, g.taps, 0)
    moved = jnp.where(jnp.abs(tap - g.q) < reached, moved, 0.0)
    levels = jnp.concatenate(
        [jnp.where(level == g.rim - j - first, moved, 0.0) for j in range(g.near)], 0
    ).astype(BF16)
    entry = iota((256, g.k * 128), 0) >> 2
    place = iota((256, g.k * 128), 1)
    offset = ((place & 127) + g.q) & 127
    wanted = (place >> 7) * g.taps + offset
    spot = ((entry == wanted) & (offset < g.taps)).astype(F32).astype(BF16)
    placed = jnp.dot(levels, spot, preferred_element_type=F32)
    for k in range(g.k):
        taps_s[k] = placed[:, k * 128 : (k + 1) * 128]

    l_in = iota((g.cols, g.cols), 0)
    l_out = iota((g.cols, g.cols), 1)
    near = jnp.abs(l_in - l_out) <= g.q
    m_in = iota((8, g.cols), 0)
    m_out = iota((8, g.cols), 1)
    from_left = m_out <= m_in
    from_right = m_out >= m_in + (g.cols - 8)

    def build(p, carry):
        for i in range(2):
            empty = (g.window - 1) * (1 - i)
            for k in range(g.k):
                lanes = slice((2 * k + i) * 128, (2 * k + i + 1) * 128)
                toep[p, empty * 128 : (empty + 1) * 128, lanes] = jnp.zeros((128, 128), BF16)
                rim_row = g.band + empty * 16
                toep[p, rim_row : rim_row + 16, lanes] = jnp.zeros((16, 128), BF16)
                for j in range(g.near):
                    row = taps_s[k, pl.ds(j * 32 + 2 * p + i + j, 1), :]
                    wheel = pltpu.roll(
                        jnp.broadcast_to(row, (128, 128)), 0, 1, stride=1, stride_axis=0
                    )
                    at = i + j
                    toep[p, at * 128 : (at + 1) * 128, lanes] = jnp.where(near, wheel, 0.0).astype(BF16)
                    corner = jnp.concatenate(
                        [
                            jnp.where(from_left, wheel[120:], 0.0),
                            jnp.where(from_right, wheel[:8], 0.0),
                        ],
                        0,
                    )
                    rim_row = g.band + at * 16
                    toep[p, rim_row : rim_row + 16, lanes] = corner.astype(BF16)
        return carry

    lax.fori_loop(0, g.pairs, build, 0)

    load_x.wait()
    load_w.wait()
    for i in range(rows):
        xt[i * 128 : (i + 1) * 128, :] = x_s[i].T
    for k in range(g.k):
        wt[:, k * g.c : (k + 1) * g.c] = w_s[k * g.c : (k + 1) * g.c, :].T

    for copy in sends:
        copy.wait()

    for w in range(tall):
        at = 16 * ((w + 1) // 2)
        odd = 8 * ((w + 1) % 2)
        rim_s[16 * w : 16 * w + 16, :] = jnp.concatenate(
            [
                left[at : at + 16, :].astype(F32)[odd : odd + 8],
                right[at : at + 16, :].astype(F32)[odd : odd + 8],
            ],
            0,
        ).astype(BF16)

    def spread(p, carry):
        wide = [cot_s[2 * p + j] for j in range(g.window)]
        ends = rim_s[pl.ds(pl.multiple_of(32 * p, 32), 16 * g.window), :]
        wide.append(ends.T)
        total = jnp.dot(jnp.concatenate(wide, 1), toep[p], preferred_element_type=F32)
        for k in range(g.k):
            sp[p, k * g.c : (k + 1) * g.c, :] = total[:, k * 256 : (k + 1) * 256].astype(BF16)
        return carry

    lax.fori_loop(0, g.pairs, spread, 0)

    def term(h, n):
        row = pl.multiple_of(h * (3 * g.chunk) + n * g.chunk, 32)
        at = pl.multiple_of(h * g.half + n * g.part, 8)
        rows_of = [sp[p, pl.ds(row, g.chunk), :] for p in range(g.pairs)]
        total = jnp.dot(jnp.concatenate(rows_of, 1), xt[...], preferred_element_type=F32)
        for b in range(g.blocks):
            grad[pl.ds(at + b * g.chunk, g.chunk), :] = total[:, b * 128 : (b + 1) * 128]

    theirs = 1 - core
    to_core = []
    for n in range(3):
        term(theirs, n)
        at = pl.multiple_of(theirs * g.half + n * g.part, 8)
        copy = remote(
            grad.at[pl.ds(at, g.part)],
            core_in.at[pl.ds(n * g.part, g.part)],
            (core_send, core_recv),
            n,
            sibling,
        )
        copy.start()
        to_core.append(copy)
    for n in range(3):
        term(core, n)
    for n in range(3):
        to_core[n].wait()
        at = pl.multiple_of(core * g.half + n * g.part, 8)
        both = grad[pl.ds(at, g.part), :] + core_in[n * g.part : (n + 1) * g.part, :]
        grad16[n * g.part : (n + 1) * g.part, :] = both.astype(BF16)
    spare = g.piece * g.xy - g.half
    if spare:
        grad16[g.half :, :] = jnp.zeros((spare, 128), BF16)

    to_xy = []
    for d in range(1, g.xy):
        peer, device = xy_peer(d)
        copy = remote(
            grad16.at[pl.ds(pl.multiple_of(peer * g.piece, 16), g.piece)],
            xy_in.at[d],
            (xy_send, xy_recv),
            d,
            device,
        )
        copy.start()
        to_xy.append(copy)

    def inward(p, carry):
        total = jnp.dot(wt[...], sp[p], preferred_element_type=F32).astype(BF16)
        out_s[2 * p] = total[:, :128]
        out_s[2 * p + 1] = total[:, 128:]
        return carry

    lax.fori_loop(0, g.pairs, inward, 0)
    store_out = pltpu.make_async_copy(out_s, out, local_sem.at[3])
    store_out.start()

    total = grad16[pl.ds(pl.multiple_of(me_xy * g.piece, 16), g.piece), :].astype(F32)
    for d in range(1, g.xy):
        to_xy[d - 1].wait()
        total = total + xy_in[d].astype(F32)
    own[: g.piece, :] = total
    spare = g.sub * g.z - g.piece
    if spare:
        own[g.piece :, :] = jnp.zeros((spare, 128), F32)

    to_z = []
    for d in range(1, g.z):
        peer, device = z_peer(d)
        copy = remote(
            own.at[pl.ds(pl.multiple_of(peer * g.sub, 16), g.sub)],
            z_in.at[d],
            (z_send, z_recv),
            d,
            device,
        )
        copy.start()
        to_z.append(copy)
    mine = pl.ds(pl.multiple_of(zi * g.sub, 16), g.sub)
    total = own[mine, :]
    for d in range(1, g.z):
        to_z[d - 1].wait()
        total = total + z_in[d]
    sub16[...] = total.astype(BF16)

    to_z = []
    for d in range(1, g.z):
        copy = remote(sub16, own16.at[mine], (zg_send, zg_recv), d, z_peer(d)[1])
        copy.start()
        to_z.append(copy)
    own16[mine, :] = sub16[...]
    for copy in to_z:
        copy.wait()

    to_xy = []
    here = pl.ds(pl.multiple_of(me_xy * g.piece, 16), g.piece)
    for d in range(1, g.xy):
        copy = remote(
            own16.at[pl.ds(0, g.piece)],
            gathered.at[core, here],
            (xyg_send, xyg_recv),
            d,
            xy_peer(d)[1],
        )
        copy.start()
        to_xy.append(copy)
    gathered[core, here, :] = own16[: g.piece, :]
    for copy in to_xy:
        copy.wait()
    swap = remote(gathered.at[core], gathered.at[core], (core_send, core_recv), 3, sibling)
    swap.start()
    swap.wait()
    store_out.wait()


def on_device(cotangent, layer_input, filter_values, weights, row_offset, reach):
    channels, rows, cols = cotangent.shape
    kernels, nlat, span, taps = filter_values.shape
    lat, lon = lax.axis_size("lat"), lax.axis_size("lon")
    g = Plan(lat, lon, channels, rows, cols, nlat, kernels, span, taps)
    entries = kernels * taps * span
    table = filter_values.transpose(0, 3, 2, 1).reshape(entries, nlat)
    table = jnp.pad(table, ((0, 256 - entries), (0, 0)))
    anywhere = pl.BlockSpec(memory_space=pl.ANY)
    vmem = pl.BlockSpec(memory_space=pltpu.VMEM)
    dma = pltpu.SemaphoreType.DMA
    field = (rows, channels, cols)
    out, gathered = pl.pallas_call(
        functools.partial(kernel, g),
        out_shape=(
            jax.ShapeDtypeStruct(field, BF16),
            jax.ShapeDtypeStruct((2, g.piece * g.xy, 128), BF16),
        ),
        in_specs=[anywhere, anywhere, anywhere, vmem, vmem, vmem],
        out_specs=(anywhere, vmem),
        scratch_shapes=[
            pltpu.VMEM((g.tall, channels, cols), BF16),
            pltpu.VMEM(field, BF16),
            pltpu.VMEM((rows * cols, channels), BF16),
            pltpu.VMEM((g.mix, channels), BF16),
            pltpu.VMEM((channels, g.mix), BF16),
            pltpu.VMEM((kernels, g.near * 32, 128), F32),
            pltpu.VMEM((g.pairs, g.deep, kernels * 256), BF16),
            pltpu.VMEM((g.pairs, g.mix, 256), BF16),
            pltpu.VMEM((8 * rows, channels), BF16),
            pltpu.VMEM((8 * rows, channels), BF16),
            pltpu.VMEM((8 * rows + 64, channels), BF16),
            pltpu.VMEM((8 * rows + 64, channels), BF16),
            pltpu.VMEM((16 * g.tall, channels), BF16),
            pltpu.VMEM((2 * g.half, 128), F32),
            pltpu.VMEM((g.half, 128), F32),
            pltpu.VMEM((g.piece * g.xy, 128), BF16),
            pltpu.VMEM((g.xy, g.piece, 128), BF16),
            pltpu.VMEM((g.sub * g.z, 128), F32),
            pltpu.VMEM((g.z, g.sub, 128), F32),
            pltpu.VMEM((g.sub, 128), BF16),
            pltpu.VMEM((g.sub * g.z, 128), BF16),
            pltpu.VMEM(field, BF16),
            dma((4,)),
            dma((8,)),
            dma((8,)),
            dma((4,)),
            dma((4,)),
            dma((g.xy,)),
            dma((g.xy,)),
            dma((g.z,)),
            dma((g.z,)),
            dma((g.z,)),
            dma((g.z,)),
            dma((g.xy,)),
            dma((g.xy,)),
        ],
        compiler_params=pltpu.CompilerParams(
            collective_id=0, has_side_effects=True, vmem_limit_bytes=56 * 2**20
        ),
    )(
        cotangent.transpose(1, 0, 2),
        layer_input.transpose(1, 0, 2),
        weights.reshape(kernels * channels, channels),
        table,
        row_offset.reshape(1, nlat),
        reach.reshape(1, nlat),
    )
    total = gathered[:, : g.half].reshape(6, g.blocks, g.chunk, 128)
    total = total.transpose(0, 2, 1, 3).reshape(kernels, channels, channels).astype(F32)
    weight_grad = total / jnp.sqrt(jnp.float32(nlat * cols * lon))
    return out.transpose(1, 0, 2), weight_grad


def solution(mesh):
    return jax.shard_map(
        on_device,
        mesh=mesh,
        in_specs=(P(None, "lat", "lon"), P(None, "lat", "lon"), P(), P(), P(), P()),
        out_specs=(P(None, "lat", "lon"), P()),
        check_vma=False,
    )
```

time: 653 us -> 67.9 us (0.10)
  waiting for transfers between devices: 267 us -> 0 us
  matrix products: 181 us -> 0 us
  local copies, waits for them, and re-layouts: 117 us -> 8.73 us
  Pallas kernels: 0 us -> 56.9 us
  blocking collectives: 48.2 us -> 0 us
  between operations: 15.5 us -> 0.66 us
  starting transfers between devices: 13.9 us -> 0 us
    psum x1 -> x0, waiting for transfers between devices: 251 us -> none  [on_device(): total_grad = lax.psum(partial_grad, ('lat', 'lon'))]
    dot_general x20 -> x0, matrix products: 181 us -> none  [the longest x17 170 us: add_tap(): jnp.einsum('kio,col->kcil', mix_tap, shifted, preferred_element_type=jnp....]
    pallas_call x0 -> x1, Pallas kernels: none -> 56.9 us  [on_device(): pl.pallas_call(functools.partial(kernel, g), out_shape=(jax.ShapeDtypeStr...]
    all_to_all x1 -> x0, blocking collectives: 48.2 us -> none  [on_device(): lax.all_to_all(tap_spread_width, 'lon', split_axis=3, concat_axis=1, tile...]
    unnamed x15 -> x3, local copies, waits for them, and re-layouts: 41 us -> 1.02 us
    all_to_all x3 -> x0, local copies, waits for them, and re-layouts: 18.7 us -> none  [the longest x1 13.7 us: on_device(): lax.all_to_all(tap_spread_width, 'lon', split_axis=3, concat_axis=1, tile...]
    convert_element_type x1 -> x0, local copies, waits for them, and re-layouts: 14.4 us -> none  [on_device(): lax.fori_loop(lower, upper, add_tap, start).astype(jnp.bfloat16)]
    all_to_all x1 -> x0, waiting for transfers between devices: 13.8 us -> none  [on_device(): lax.all_to_all(padded, 'lon', split_axis=0, concat_axis=2, tiled=True)]
  transfers between devices with their start and end apart: 4 -> 0, of which waited for: 3 -> 0; matrix products, arithmetic and copies ran while one was open for 3% -> 0% of each run, Pallas kernels for 0% -> 0%
where the time goes in v1:
time: 67.9 us; the launch traced here: 67.6 us
  Pallas kernels  56.9 us (84%)
  local copies, waits for them, and re-layouts  8.73 us (13%)
  other arithmetic  1.31 us (2%)
    pallas_call x1, Pallas kernels, on_device(): pl.pallas_call(functools.partial(kernel, g), out_shape=(jax.ShapeDtypeStr...  56.9 us
    div x2, local copies, waits for them, and re-layouts, on_device(): weight_grad = total / jnp.sqrt(jnp.float32(nlat * cols * lon))  3.49 us

profile of v1, /device:TPU:1, one launch (start us, length us, event | category | flops | bytes accessed | tf_op | source)
XLA Modules:
  0.0 67.6 jit_solution(8188448971184582838)
XLA Ops:
  0.6 1.2 %reshape.26.ro = s32[1,384]{1,0:T(1,128)} reshape(s32[384]{0:T(512)} %param.10) | data formatting | bytes 3072 | tf_op jit(solution)/shard_map/reshape | solution.py:455
  1.9 1.3 %reshape.27.reach = s32[1,384]{1,0:T(1,128)} reshape(s32[384]{0:T(512)} %param.11) | data formatting | bytes 3072 | tf_op jit(solution)/shard_map/reshape | solution.py:456
  3.2 1.0 %reshape.25 = bf16[204,384]{1,0:T(8,128)(2,1)S(1)} reshape(bf16[3,17,4,384]{3,2,1,0:T(4,128)(2,1)} %bitcast.15) | data formatting | bytes 313344 | tf_op jit(solution)/shard_map/reshape | solution.py:396
  4.2 0.7 %pad.4.fv = bf16[256,384]{1,0:T(8,128)(2,1)} pad(bf16[204,384]{1,0:T(8,128)(2,1)S(1)} %reshape.25, bf16[]{:T(256)} %constant.4.clone.1), padding=0_52x0_0 | pad | bytes 353282 | tf_op jit(solution)/shard_map/jit(_pad)/pad | solution.py:397
  4.9 56.9 %shard_map.77 = (bf16[12,384,128]{2,1,0:T(8,128)(2,1)}, bf16[2,1792,128]{2,1,0:T(8,128)(2,1)}) custom-call(bf16[12,384,128]{2,1,0:T(8,128)(2,1)} %bitcast.11, bf16[12,384,128]{2,1,0:T(8,128)(2,1)} %bitcast.12, bf16[1152,384]{1,0:T(8,128)(2,1)} %bitcast.14, bf16[256,384]{1,0:T(8,128)(2,1)} %pad.4.fv, s32[1,384]{1,0:T(1,128)} %reshape.26.ro, ...), custom_call_target="tpu_custom_call" | custom-call | tf_op jit(solution)/shard_map/pallas_call | solution.py:402
  61.8 1.3 %convert_multiply_fusion = f32[2,1728,128]{2,1,0:T(8,128)S(1)} fusion(bf16[2,1792,128]{2,1,0:T(8,128)(2,1)} %get-tuple-element.5), kind=kLoop, calls=%fused_computation.1 | loop fusion | flops 884736 | bytes 2654208 | tf_op jit(solution)/shard_map/div | solution.py:460
  63.1 1.2 %copy.11 = f32[6,3,192,128]{3,1,2,0:T(4,128)S(1)} copy(f32[6,3,192,128]{3,2,1,0:T(8,128)S(1)} %bitcast.10) | data formatting | bytes 3538944 | tf_op jit(solution)/shard_map/div | solution.py:460
  64.3 0.0 copy-start
  64.3 2.3 %div.16 = f32[3,384,384]{2,1,0:T(8,128)} reshape(f32[6,192,3,128]{3,2,1,0:T(4,128)S(1)} %bitcast.9) | data formatting | bytes 3538944 | tf_op jit(solution)/shard_map/div | solution.py:460
  66.6 0.0 copy-done
  66.6 1.0 %copy.13 = bf16[384,12,128]{2,0,1:T(8,128)(2,1)} copy(bf16[384,12,128]{2,0,1:T(8,128)(2,1)S(1)} %bitcast.13) | data formatting | bytes 2359296
Async XLA Ops:
  64.3 2.3 %copy-start = (bf16[12,384,128]{2,1,0:T(8,128)(2,1)S(1)}, bf16[12,384,128]{2,1,0:T(8,128)(2,1)}, u32[]{:S(2)}) copy-start(bf16[12,384,128]{2,1,0:T(8,128)(2,1)} %get-tuple-element.4) | copy-start | bytes 3538948

commit v2 on v1

v2 whole, which is shorter than its diff:
```python
import functools
import math

import jax
import jax.numpy as jnp
from jax import lax
from jax.experimental import pallas as pl
from jax.experimental.pallas import tpu as pltpu
from jax.sharding import PartitionSpec as P

MESH = pl.DeviceIdType.MESH
F32 = jnp.float32
BF16 = jnp.bfloat16


def iota(shape, dim):
    return lax.broadcasted_iota(jnp.int32, shape, dim)


def ceil_to(n, m):
    return -(-n // m) * m


class Plan:
    def __init__(self, lat, lon, channels, rows, cols, nlat, kernels, span, taps):
        self.lat, self.lon = lat, lon
        self.c, self.rows, self.cols = channels, rows, cols
        self.nlat, self.k, self.span, self.taps = nlat, kernels, span, taps
        self.q = (taps - 1) // 2
        self.rim = span - 1
        self.tall = rows + 2 * self.rim
        self.near = 2 * span - 1
        self.pairs = rows // 2
        self.window = self.near + 1
        self.band = self.window * cols
        self.deep = self.band + self.window * 16
        self.mix = kernels * channels
        self.scale = 1.0 / math.sqrt(nlat * cols * lon)
        self.z = lat // 4
        self.far = self.z // 2
        self.team = 4 * lon
        self.chunks = 2
        self.wide = channels // self.chunks
        self.slim = self.wide // 2
        self.tier = kernels * self.slim
        self.blocks = channels // 128
        self.half = self.blocks * self.tier
        self.piece = ceil_to(-(-self.half // self.team), 16)
        self.owners = self.half // self.piece
        self.idle = self.team - self.owners


def remote(src, dst, sems, n, device):
    return pltpu.make_async_remote_copy(
        src_ref=src,
        dst_ref=dst,
        send_sem=sems[0].at[n],
        recv_sem=sems[1].at[n],
        device_id=device,
        device_id_type=MESH,
    )


def kernel(
    g,
    cot,
    xin,
    w_in,
    fv,
    ro,
    reach,
    out,
    total_out,
    cot_s,
    x_s,
    xt,
    w_s,
    wt,
    table,
    taps_s,
    toep,
    sp,
    pack_l,
    pack_r,
    left,
    right,
    rim_s,
    rim_t,
    grad,
    core_in,
    grad16,
    team_in,
    far_in,
    final,
    gathered,
    out_s,
    local_sem,
    halo_send,
    halo_recv,
    core_send,
    core_recv,
    team_send,
    team_recv,
    far_send,
    far_recv,
    back_send,
    back_recv,
):
    lat = lax.axis_index("lat")
    lon = lax.axis_index("lon")
    core = lax.rem(lat, 2)
    zi = lax.rem(lat // 2, g.z)
    ylo = lat // (2 * g.z)
    z_lo, z_hi = lax.rem(zi, 2), zi // 2
    me = (ylo * g.lon + lon) * 2 + z_lo
    up, down = lax.rem(lat + 1, g.lat), lax.rem(lat + g.lat - 1, g.lat)
    east, west = lax.rem(lon + 1, g.lon), lax.rem(lon + g.lon - 1, g.lon)
    sibling = (lat + 1 - 2 * core, lon)

    def team_peer(d):
        peer = lax.rem(me + d, g.team)
        column = peer // 2
        z = 2 * z_hi + lax.rem(peer, 2)
        return peer, ((column // g.lon) * (2 * g.z) + 2 * z + core, lax.rem(column, g.lon))

    def far_peer(d):
        z = 2 * lax.rem(z_hi + d, g.far) + z_lo
        return (ylo * 2 * g.z + 2 * z + core, lon)

    halo = [
        (up, east),
        (up, west),
        (down, east),
        (down, west),
        (lat, east),
        (lat, west),
        (up, lon),
        (down, lon),
    ]
    partners = halo + [sibling]
    partners += [team_peer(d)[1] for d in range(1, g.team)]
    partners += [far_peer(d) for d in range(1, g.far)]

    barrier = pltpu.get_barrier_semaphore()
    for peer in partners:
        pl.semaphore_signal(barrier, inc=1, device_id=peer, device_id_type=MESH)

    load_cot = pltpu.make_async_copy(cot, cot_s.at[pl.ds(g.rim, g.rows)], local_sem.at[0])
    load_x = pltpu.make_async_copy(xin, x_s, local_sem.at[1])
    load_w = pltpu.make_async_copy(w_in, w_s, local_sem.at[2])
    load_cot.start()
    load_x.start()
    load_w.start()
    load_cot.wait()

    pick = iota((16, g.cols), 0)
    lane = iota((16, g.cols), 1)
    pick = (lane == jnp.where(pick < 8, pick + (g.cols - 8), pick - 8)).astype(F32).astype(BF16)
    for o in range(0, g.rows, 2):
        edge = [
            lax.dot_general(
                pick, cot_s[g.rim + o + n], (((1,), (1,)), ((), ())), preferred_element_type=F32
            )
            for n in range(2)
        ]
        pack_r[8 * o : 8 * o + 16, :] = jnp.concatenate([edge[0][:8], edge[1][:8]], 0).astype(BF16)
        pack_l[8 * o : 8 * o + 16, :] = jnp.concatenate([edge[0][8:], edge[1][8:]], 0).astype(BF16)

    pl.semaphore_wait(barrier, len(partners))

    sems = (halo_send, halo_recv)
    n_own = 8 * g.rows
    last = n_own - 32
    rim, tall, rows = g.rim, g.tall, g.rows
    sends = [
        remote(pack_r.at[pl.ds(last, 32)], left.at[pl.ds(0, 32)], sems, 0, halo[0]),
        remote(pack_l.at[pl.ds(last, 32)], right.at[pl.ds(0, 32)], sems, 1, halo[1]),
        remote(pack_r.at[pl.ds(0, 32)], left.at[pl.ds(32 + n_own, 32)], sems, 2, halo[2]),
        remote(pack_l.at[pl.ds(0, 32)], right.at[pl.ds(32 + n_own, 32)], sems, 3, halo[3]),
        remote(pack_r, left.at[pl.ds(32, n_own)], sems, 4, halo[4]),
        remote(pack_l, right.at[pl.ds(32, n_own)], sems, 5, halo[5]),
        remote(cot.at[pl.ds(rows - rim, rim)], cot_s.at[pl.ds(0, rim)], sems, 6, halo[6]),
        remote(cot.at[pl.ds(0, rim)], cot_s.at[pl.ds(tall - rim, rim)], sems, 7, halo[7]),
    ]
    for copy in sends:
        copy.start()

    entries = g.k * g.taps * g.span
    for k in range(g.k):
        for t in range(g.taps):
            n = (k * g.taps + t) * g.span
            table[n : n + g.span, :] = fv[k, t].astype(F32)
    table[entries:, :] = jnp.zeros((256 - entries, g.nlat), F32)
    source = iota((32, g.nlat), 1)
    slot = iota((32, g.nlat), 0)
    here = (source == lat * rows - rim + slot) & (slot < tall)
    moved = lax.dot_general(
        here.astype(F32).astype(BF16),
        table[...].astype(BF16),
        (((1,), (1,)), ((), ())),
        preferred_element_type=F32,
    )
    first = jnp.where(here, ro[...].astype(F32)[None, :], 0.0)
    first = jnp.sum(first, axis=1, keepdims=True).astype(jnp.int32)
    reached = jnp.where(here, reach[...].astype(F32)[None, :], 0.0)
    reached = jnp.sum(reached, axis=1, keepdims=True).astype(jnp.int32)
    column = iota((32, 256), 1)
    level = column & 3
    order = column >> 2
    tap = order
    for n in range(1, g.k):
        tap = tap - jnp.where(order >= n * g.taps, g.taps, 0)
    moved = jnp.where(jnp.abs(tap - g.q) < reached, moved, 0.0)
    levels = jnp.concatenate(
        [jnp.where(level == g.rim - j - first, moved, 0.0) for j in range(g.near)], 0
    ).astype(BF16)
    entry = iota((256, g.k * 128), 0) >> 2
    place = iota((256, g.k * 128), 1)
    offset = ((place & 127) + g.q) & 127
    wanted = (place >> 7) * g.taps + offset
    spot = ((entry == wanted) & (offset < g.taps)).astype(F32).astype(BF16)
    placed = jnp.dot(levels, spot, preferred_element_type=F32)
    for k in range(g.k):
        taps_s[k] = placed[:, k * 128 : (k + 1) * 128]

    l_in = iota((g.cols, g.cols), 0)
    l_out = iota((g.cols, g.cols), 1)
    near = jnp.abs(l_in - l_out) <= g.q
    m_in = iota((8, g.cols), 0)
    m_out = iota((8, g.cols), 1)
    from_left = m_out <= m_in
    from_right = m_out >= m_in + (g.cols - 8)

    def build(p, carry):
        for i in range(2):
            empty = (g.window - 1) * (1 - i)
            for k in range(g.k):
                lanes = slice((2 * k + i) * 128, (2 * k + i + 1) * 128)
                toep[p, empty * 128 : (empty + 1) * 128, lanes] = jnp.zeros((128, 128), BF16)
                rim_row = g.band + empty * 16
                toep[p, rim_row : rim_row + 16, lanes] = jnp.zeros((16, 128), BF16)
                for j in range(g.near):
                    row = taps_s[k, pl.ds(j * 32 + 2 * p + i + j, 1), :]
                    wheel = pltpu.roll(
                        jnp.broadcast_to(row, (128, 128)), 0, 1, stride=1, stride_axis=0
                    )
                    at = i + j
                    toep[p, at * 128 : (at + 1) * 128, lanes] = jnp.where(near, wheel, 0.0).astype(BF16)
                    corner = jnp.concatenate(
                        [
                            jnp.where(from_left, wheel[120:], 0.0),
                            jnp.where(from_right, wheel[:8], 0.0),
                        ],
                        0,
                    )
                    rim_row = g.band + at * 16
                    toep[p, rim_row : rim_row + 16, lanes] = corner.astype(BF16)
        return carry

    lax.fori_loop(0, g.pairs, build, 0)

    load_x.wait()
    load_w.wait()
    for i in range(rows):
        xt[i * 128 : (i + 1) * 128, :] = x_s[i].T
    for k in range(g.k):
        wt[:, k * g.c : (k + 1) * g.c] = w_s[k * g.c : (k + 1) * g.c, :].T

    for copy in sends:
        copy.wait()

    for w in range(tall):
        at = 16 * ((w + 1) // 2)
        odd = 8 * ((w + 1) % 2)
        rim_s[16 * w : 16 * w + 16, :] = jnp.concatenate(
            [
                left[at : at + 16, :].astype(F32)[odd : odd + 8],
                right[at : at + 16, :].astype(F32)[odd : odd + 8],
            ],
            0,
        ).astype(BF16)

    def spread(m):
        part = slice(m * g.wide, (m + 1) * g.wide)

        def step(p, carry):
            wide = [cot_s[2 * p + j, part, :] for j in range(g.window)]
            if m == 0:
                ends = rim_s[pl.ds(pl.multiple_of(32 * p, 32), 16 * g.window), :].T
                rim_t[p] = ends
                wide.append(ends[part])
            else:
                wide.append(rim_t[p, part, :])
            total = jnp.dot(jnp.concatenate(wide, 1), toep[p], preferred_element_type=F32)
            for k in range(g.k):
                at = k * g.c + m * g.wide
                sp[p, at : at + g.wide, :] = total[:, k * 256 : (k + 1) * 256].astype(BF16)
            return carry

        lax.fori_loop(0, g.pairs, step, 0)

    def term(m, h):
        tiers = []
        for k in range(g.k):
            at = pl.multiple_of(k * g.c + m * g.wide + h * g.slim, 32)
            tiers.append(
                jnp.concatenate([sp[p, pl.ds(at, g.slim), :] for p in range(g.pairs)], 1)
            )
        return jnp.dot(jnp.concatenate(tiers, 0), xt[...], preferred_element_type=F32)

    to_core = [
        remote(grad.at[m], core_in.at[m], (core_send, core_recv), m, sibling)
        for m in range(g.chunks)
    ]

    def give(m):
        total = term(m, 1 - core)
        for b in range(g.blocks):
            grad[m, b * g.tier : (b + 1) * g.tier, :] = total[:, b * 128 : (b + 1) * 128]
        to_core[m].start()

    def keep(m):
        total = term(m, core)
        to_core[m].wait()
        for b in range(g.blocks):
            at = slice(b * g.tier, (b + 1) * g.tier)
            both = total[:, b * 128 : (b + 1) * 128] + core_in[m, at, :]
            grad16[m, at, :] = both.astype(BF16)

    def owned(index, m):
        n = index - m * g.idle
        return n, (n >= 0) & (n < g.owners)

    def rows_of(n):
        return pl.ds(pl.multiple_of(n * g.piece, 16), g.piece)

    def to_owner(m, d):
        peer, device = team_peer(d)
        n, valid = owned(peer, m)
        n = jnp.where(valid, n, 0)
        sems = (team_send, team_recv)
        at = team_in.at[m, d]
        return valid, remote(grad16.at[m, rows_of(n)], at, sems, m * g.team + d, device)

    def scatter(m):
        for d in range(1, g.team):
            valid, copy = to_owner(m, d)

            @pl.when(valid)
            def _():
                copy.start()

    def to_far(m, d):
        sems = (far_send, far_recv)
        here = far_in.at[m, z_hi]
        return remote(here, here, sems, m * g.far + d, far_peer(d))

    def add(m):
        n, mine = owned(me, m)

        @pl.when(mine)
        def _():
            total = grad16[m, rows_of(n), :].astype(F32)
            for d in range(1, g.team):
                to_owner(m, d)[1].wait_recv()
                total = total + team_in[m, d].astype(F32)
            far_in[m, z_hi] = total
            for d in range(1, g.far):
                to_far(m, d).start()

        for d in range(1, g.team):
            valid, copy = to_owner(m, d)

            @pl.when(valid)
            def _():
                copy.wait_send()

    def from_owner(m, d):
        n, _ = owned(me, m)
        there = gathered.at[m, core, rows_of(n)]
        sems = (back_send, back_recv)
        return remote(final.at[m], there, sems, m * g.team + d, team_peer(d)[1])

    def finish(m):
        n, mine = owned(me, m)

        @pl.when(mine)
        def _():
            for d in range(1, g.far):
                to_far(m, d).wait()
            total = far_in[m, 0]
            for f in range(1, g.far):
                total = total + far_in[m, f]
            final[m] = total.astype(BF16)
            for d in range(1, g.team):
                from_owner(m, d).start()
            gathered[m, core, rows_of(n), :] = final[m]

    swaps = [
        remote(
            gathered.at[m, core],
            gathered.at[m, core],
            (core_send, core_recv),
            g.chunks + m,
            sibling,
        )
        for m in range(g.chunks)
    ]

    def collect(m):
        n, mine = owned(me, m)
        for d in range(1, g.team):
            sender = lax.rem(me + g.team - d, g.team)
            valid = owned(sender, m)[1]
            sems = (back_send, back_recv)
            there = gathered.at[m, core, pl.ds(0, g.piece)]
            copy = remote(final.at[m], there, sems, m * g.team + d, team_peer(d)[1])

            @pl.when(valid)
            def _():
                copy.wait_recv()

        swaps[m].start()

        @pl.when(mine)
        def _():
            for d in range(1, g.team):
                from_owner(m, d).wait_send()

    def unfold(m):
        swaps[m].wait()
        for h in range(2):
            for k in range(g.k):
                at = k * g.c + m * g.wide + h * g.slim
                for b in range(g.blocks):
                    row = b * g.tier + k * g.slim
                    piece = gathered[m, h, row : row + g.slim, :].astype(F32) * g.scale
                    total_out[at : at + g.slim, b * 128 : (b + 1) * 128] = piece

    def inward(p, carry):
        total = jnp.dot(wt[...], sp[p], preferred_element_type=F32).astype(BF16)
        out_s[2 * p] = total[:, :128]
        out_s[2 * p + 1] = total[:, 128:]
        return carry

    spread(0)
    give(0)
    spread(1)
    give(1)
    keep(0)
    scatter(0)
    keep(1)
    scatter(1)
    lax.fori_loop(0, g.pairs, inward, 0)
    store_out = pltpu.make_async_copy(out_s, out, local_sem.at[3])
    store_out.start()
    add(0)
    add(1)
    finish(0)
    finish(1)
    collect(0)
    collect(1)
    unfold(0)
    unfold(1)
    store_out.wait()


def on_device(cotangent, layer_input, filter_values, weights, row_offset, reach):
    channels, rows, cols = cotangent.shape
    kernels, nlat, span, taps = filter_values.shape
    lat, lon = lax.axis_size("lat"), lax.axis_size("lon")
    g = Plan(lat, lon, channels, rows, cols, nlat, kernels, span, taps)
    anywhere = pl.BlockSpec(memory_space=pl.ANY)
    vmem = pl.BlockSpec(memory_space=pltpu.VMEM)
    dma = pltpu.SemaphoreType.DMA
    field = (rows, channels, cols)
    chunks = g.chunks
    out, total = pl.pallas_call(
        functools.partial(kernel, g),
        out_shape=(
            jax.ShapeDtypeStruct(field, BF16),
            jax.ShapeDtypeStruct((g.mix, channels), F32),
        ),
        in_specs=[anywhere, anywhere, anywhere, vmem, vmem, vmem],
        out_specs=(anywhere, vmem),
        scratch_shapes=[
            pltpu.VMEM((g.tall, channels, cols), BF16),
            pltpu.VMEM(field, BF16),
            pltpu.VMEM((rows * cols, channels), BF16),
            pltpu.VMEM((g.mix, channels), BF16),
            pltpu.VMEM((channels, g.mix), BF16),
            pltpu.VMEM((256, nlat), F32),
            pltpu.VMEM((kernels, g.near * 32, 128), F32),
            pltpu.VMEM((g.pairs, g.deep, kernels * 256), BF16),
            pltpu.VMEM((g.pairs, g.mix, 256), BF16),
            pltpu.VMEM((8 * rows, channels), BF16),
            pltpu.VMEM((8 * rows, channels), BF16),
            pltpu.VMEM((8 * rows + 64, channels), BF16),
            pltpu.VMEM((8 * rows + 64, channels), BF16),
            pltpu.VMEM((16 * g.tall, channels), BF16),
            pltpu.VMEM((g.pairs, channels, 128), BF16),
            pltpu.VMEM((chunks, g.half, 128), F32),
            pltpu.VMEM((chunks, g.half, 128), F32),
            pltpu.VMEM((chunks, g.half, 128), BF16),
            pltpu.VMEM((chunks, g.team, g.piece, 128), BF16),
            pltpu.VMEM((chunks, g.far, g.piece, 128), F32),
            pltpu.VMEM((chunks, g.piece, 128), BF16),
            pltpu.VMEM((chunks, 2, g.half, 128), BF16),
            pltpu.VMEM(field, BF16),
            dma((4,)),
            dma((8,)),
            dma((8,)),
            dma((2 * chunks,)),
            dma((2 * chunks,)),
            dma((chunks * g.team,)),
            dma((chunks * g.team,)),
            dma((chunks * g.far,)),
            dma((chunks * g.far,)),
            dma((chunks * g.team,)),
            dma((chunks * g.team,)),
        ],
        compiler_params=pltpu.CompilerParams(
            collective_id=0, has_side_effects=True, vmem_limit_bytes=56 * 2**20
        ),
    )(
        cotangent.transpose(1, 0, 2),
        layer_input.transpose(1, 0, 2),
        weights.reshape(kernels * channels, channels),
        filter_values.transpose(0, 3, 2, 1),
        row_offset,
        reach,
    )
    return out.transpose(1, 0, 2), total.reshape(kernels, channels, channels)


def solution(mesh):
    return jax.shard_map(
        on_device,
        mesh=mesh,
        in_specs=(P(None, "lat", "lon"), P(None, "lat", "lon"), P(), P(), P(), P()),
        out_specs=(P(None, "lat", "lon"), P()),
        check_vma=False,
    )
```

time: 67.9 us -> 57.4 us (0.85)
  local copies, waits for them, and re-layouts: 8.73 us -> 3.7 us
  Pallas kernels: 56.9 us -> 52.9 us
  other arithmetic: 1.31 us -> 0 us
    pallas_call x1, Pallas kernels: 56.9 us -> 52.9 us  [on_device(): pl.pallas_call(functools.partial(kernel, g), out_shape=(jax.ShapeDtypeStr...]
    reshape x3 -> x0, local copies, waits for them, and re-layouts: 3.52 us -> none  [the longest x1 1.28 us: on_device(): reach.reshape(1, nlat)]
    div x2 -> x0, local copies, waits for them, and re-layouts: 3.49 us -> none  [on_device(): weight_grad = total / jnp.sqrt(jnp.float32(nlat * cols * lon))]
    unnamed x3 -> x4, local copies, waits for them, and re-layouts: 1.02 us -> 3.7 us
    div x1 -> x0, other arithmetic: 1.31 us -> none  [on_device(): weight_grad = total / jnp.sqrt(jnp.float32(nlat * cols * lon))]
    pad x1 -> x0, local copies, waits for them, and re-layouts: 0.7 us -> none  [on_device(): table = jnp.pad(table, ((0, 256 - entries), (0, 0)))]
where the time goes in v2:
time: 57.4 us; the launch traced here: 57.3 us
  Pallas kernels  52.9 us (92%)
  local copies, waits for them, and re-layouts  3.7 us (6%)
  between operations  0.65 us (1%)
    pallas_call x1, Pallas kernels, on_device(): pl.pallas_call(functools.partial(kernel, g), out_shape=(jax.ShapeDtypeStr...  52.9 us
    unnamed x4, local copies, waits for them, and re-layouts  3.7 us

profile of v2, /device:TPU:1, one launch (start us, length us, event | category | flops | bytes accessed | tf_op | source)
XLA Modules:
  0.0 57.3 jit_solution(3427754394098084214)
XLA Ops:
  0.6 52.9 %shard_map.77 = (bf16[12,384,128]{2,1,0:T(8,128)(2,1)}, f32[1152,384]{1,0:T(8,128)}) custom-call(bf16[12,384,128]{2,1,0:T(8,128)(2,1)} %bitcast.7, bf16[12,384,128]{2,1,0:T(8,128)(2,1)} %bitcast.8, bf16[1152,384]{1,0:T(8,128)(2,1)} %bitcast.10, bf16[3,17,4,384]{3,2,1,0:T(4,128)(2,1)} %bitcast.11, s32[384]{0:T(512)} %ro.1, s32[384]{0:T(512)} %reach.1), custom_call_target="tpu_custom_call" | custom-call | tf_op jit(solution)/shard_map/pallas_call | solution.py:478
  53.6 0.0 copy-start
  53.6 2.5 %copy.10 = bf16[384,12,128]{2,0,1:T(8,128)(2,1)} copy(bf16[384,12,128]{2,0,1:T(8,128)(2,1)} %bitcast.9) | data formatting | bytes 2359296
  56.1 0.0 copy-done
  56.1 1.2 %copy.11 = f32[3,384,384]{2,1,0:T(8,128)} copy(f32[3,384,384]{2,1,0:T(8,128)S(1)} %bitcast.6) | data formatting | bytes 3538944
Async XLA Ops:
  53.6 2.5 %copy-start = (f32[1152,384]{1,0:T(8,128)S(1)}, f32[1152,384]{1,0:T(8,128)}, u32[]{:S(2)}) copy-start(f32[1152,384]{1,0:T(8,128)} %get-tuple-element.5) | copy-start | bytes 5308420

commit v3 on v2

--- a/solution.py
+++ b/solution.py
@@ -1,5 +1,4 @@
 import functools
-import math
 
 import jax
 import jax.numpy as jnp
@@ -35,7 +34,6 @@
         self.band = self.window * cols
         self.deep = self.band + self.window * 16
         self.mix = kernels * channels
-        self.scale = 1.0 / math.sqrt(nlat * cols * lon)
         self.z = lat // 4
         self.far = self.z // 2
         self.team = 4 * lon
@@ -79,6 +77,7 @@
     table,
     taps_s,
     toep,
+    inner,
     sp,
     pack_l,
     pack_r,
@@ -92,7 +91,6 @@
     team_in,
     far_in,
     final,
-    gathered,
     out_s,
     local_sem,
     halo_send,
@@ -232,20 +230,29 @@
     from_right = m_out >= m_in + (g.cols - 8)
 
     def build(p, carry):
+        early = p < g.pairs // 2
+        band = jnp.where(early, g.window * 16, 0)
+        ends = jnp.where(early, 0, g.band)
+
+        def band_at(at):
+            return pl.ds(pl.multiple_of(band + at * 128, 128), 128)
+
+        def ends_at(at):
+            return pl.ds(pl.multiple_of(ends + at * 16, 16), 16)
+
         for i in range(2):
             empty = (g.window - 1) * (1 - i)
             for k in range(g.k):
                 lanes = slice((2 * k + i) * 128, (2 * k + i + 1) * 128)
-                toep[p, empty * 128 : (empty + 1) * 128, lanes] = jnp.zeros((128, 128), BF16)
-                rim_row = g.band + empty * 16
-                toep[p, rim_row : rim_row + 16, lanes] = jnp.zeros((16, 128), BF16)
+                toep[p, band_at(empty), lanes] = jnp.zeros((128, 128), BF16)
+                toep[p, ends_at(empty), lanes] = jnp.zeros((16, 128), BF16)
                 for j in range(g.near):
                     row = taps_s[k, pl.ds(j * 32 + 2 * p + i + j, 1), :]
                     wheel = pltpu.roll(
                         jnp.broadcast_to(row, (128, 128)), 0, 1, stride=1, stride_axis=0
                     )
                     at = i + j
-                    toep[p, at * 128 : (at + 1) * 128, lanes] = jnp.where(near, wheel, 0.0).astype(BF16)
+                    toep[p, band_at(at), lanes] = jnp.where(near, wheel, 0.0).astype(BF16)
                     corner = jnp.concatenate(
                         [
                             jnp.where(from_left, wheel[120:], 0.0),
@@ -253,11 +260,20 @@
                         ],
                         0,
                     )
-                    rim_row = g.band + at * 16
-                    toep[p, rim_row : rim_row + 16, lanes] = corner.astype(BF16)
+                    toep[p, ends_at(at), lanes] = corner.astype(BF16)
         return carry
 
     lax.fori_loop(0, g.pairs, build, 0)
+
+    def own_rows(p):
+        return max(0, rim - 2 * p), min(g.window, rim + rows - 2 * p)
+
+    for p in range(g.pairs):
+        low, high = own_rows(p)
+        start = g.window * 16 if p < g.pairs // 2 else 0
+        wide = jnp.concatenate([cot_s[2 * p + j] for j in range(low, high)], 1)
+        deep = toep[p, start + low * 128 : start + high * 128, :]
+        inner[p] = jnp.dot(wide, deep, preferred_element_type=F32)
 
     load_x.wait()
     load_w.wait()
@@ -266,10 +282,7 @@
     for k in range(g.k):
         wt[:, k * g.c : (k + 1) * g.c] = w_s[k * g.c : (k + 1) * g.c, :].T
 
-    for copy in sends:
-        copy.wait()
-
-    for w in range(tall):
+    def lay_rim(w):
         at = 16 * ((w + 1) // 2)
         odd = 8 * ((w + 1) % 2)
         rim_s[16 * w : 16 * w + 16, :] = jnp.concatenate(
@@ -280,24 +293,43 @@
             0,
         ).astype(BF16)
 
-    def spread(m):
-        part = slice(m * g.wide, (m + 1) * g.wide)
-
-        def step(p, carry):
-            wide = [cot_s[2 * p + j, part, :] for j in range(g.window)]
+    def spread(p, part):
+        low, high = own_rows(p)
+        ends = rim_t[p, part, :]
+        if p < g.pairs // 2:
+            wide = [ends] + [cot_s[2 * p + j, part, :] for j in range(low)]
+            deep = toep[p, : g.window * 16 + low * 128, :]
+        else:
+            wide = [cot_s[2 * p + j, part, :] for j in range(high, g.window)] + [ends]
+            deep = toep[p, high * 128 :, :]
+        total = jnp.dot(jnp.concatenate(wide, 1), deep, preferred_element_type=F32)
+        total = total + inner[p, part, :]
+        for k in range(g.k):
+            at = slice(k * g.c + part.start, k * g.c + part.stop)
+            sp[p, at, :] = total[:, k * 256 : (k + 1) * 256].astype(BF16)
+
+    def turn(p):
+        rim_t[p] = rim_s[32 * p : 32 * p + 16 * g.window, :].T
+
+    whole = [p for p in range(g.pairs) if own_rows(p) == (0, g.window)]
+    others = [p for p in range(g.pairs) if p not in whole]
+    for n in (4, 5):
+        sends[n].wait()
+    for w in range(rim + 1, tall - rim - 1):
+        lay_rim(w)
+    for p in whole:
+        turn(p)
+        spread(p, slice(0, g.c))
+    for n in (0, 1, 2, 3, 6, 7):
+        sends[n].wait()
+    for w in list(range(rim + 1)) + list(range(tall - rim - 1, tall)):
+        lay_rim(w)
+
+    def chunk(m):
+        for p in others:
             if m == 0:
-                ends = rim_s[pl.ds(pl.multiple_of(32 * p, 32), 16 * g.window), :].T
-                rim_t[p] = ends
-                wide.append(ends[part])
-            else:
-                wide.append(rim_t[p, part, :])
-            total = jnp.dot(jnp.concatenate(wide, 1), toep[p], preferred_element_type=F32)
-            for k in range(g.k):
-                at = k * g.c + m * g.wide
-                sp[p, at : at + g.wide, :] = total[:, k * 256 : (k + 1) * 256].astype(BF16)
-            return carry
-
-        lax.fori_loop(0, g.pairs, step, 0)
+                turn(p)
+            spread(p, slice(m * g.wide, (m + 1) * g.wide))
 
     def term(m, h):
         tiers = []
@@ -375,11 +407,22 @@
             def _():
                 copy.wait_send()
 
+    def landing(m, n):
+        b, r = n // (g.tier // g.piece), lax.rem(n, g.tier // g.piece)
+        k, r = r // (g.slim // g.piece), lax.rem(r, g.slim // g.piece)
+        row = k * g.c + m * g.wide + core * g.slim + r * g.piece
+        return total_out.at[
+            pl.ds(pl.multiple_of(row, 32), g.piece), pl.ds(pl.multiple_of(b * 128, 128), 128)
+        ]
+
     def from_owner(m, d):
-        n, _ = owned(me, m)
-        there = gathered.at[m, core, rows_of(n)]
+        there = landing(m, owned(me, m)[0])
         sems = (back_send, back_recv)
         return remote(final.at[m], there, sems, m * g.team + d, team_peer(d)[1])
+
+    def lay_own(m):
+        there = landing(m, owned(me, m)[0])
+        return pltpu.make_async_copy(final.at[m], there, local_sem.at[4 + m])
 
     def finish(m):
         n, mine = owned(me, m)
@@ -394,48 +437,38 @@
             final[m] = total.astype(BF16)
             for d in range(1, g.team):
                 from_owner(m, d).start()
-            gathered[m, core, rows_of(n), :] = final[m]
-
-    swaps = [
-        remote(
-            gathered.at[m, core],
-            gathered.at[m, core],
-            (core_send, core_recv),
-            g.chunks + m,
-            sibling,
-        )
-        for m in range(g.chunks)
-    ]
+            lay_own(m).start()
+
+    def swap(m, k):
+        row = pl.multiple_of(k * g.c + m * g.wide + core * g.slim, 32)
+        block = total_out.at[pl.ds(row, g.slim)]
+        sems = (core_send, core_recv)
+        return remote(block, block, sems, g.chunks + m * g.k + k, sibling)
 
     def collect(m):
-        n, mine = owned(me, m)
+        _, mine = owned(me, m)
         for d in range(1, g.team):
             sender = lax.rem(me + g.team - d, g.team)
-            valid = owned(sender, m)[1]
+            n, valid = owned(sender, m)
+            n = jnp.where(valid, n, 0)
             sems = (back_send, back_recv)
-            there = gathered.at[m, core, pl.ds(0, g.piece)]
-            copy = remote(final.at[m], there, sems, m * g.team + d, team_peer(d)[1])
+            copy = remote(final.at[m], landing(m, n), sems, m * g.team + d, team_peer(d)[1])
 
             @pl.when(valid)
             def _():
                 copy.wait_recv()
 
-        swaps[m].start()
+        @pl.when(mine)
+        def _():
+            lay_own(m).wait()
+
+        for k in range(g.k):
+            swap(m, k).start()
 
         @pl.when(mine)
         def _():
             for d in range(1, g.team):
                 from_owner(m, d).wait_send()
-
-    def unfold(m):
-        swaps[m].wait()
-        for h in range(2):
-            for k in range(g.k):
-                at = k * g.c + m * g.wide + h * g.slim
-                for b in range(g.blocks):
-                    row = b * g.tier + k * g.slim
-                    piece = gathered[m, h, row : row + g.slim, :].astype(F32) * g.scale
-                    total_out[at : at + g.slim, b * 128 : (b + 1) * 128] = piece
 
     def inward(p, carry):
         total = jnp.dot(wt[...], sp[p], preferred_element_type=F32).astype(BF16)
@@ -443,9 +476,9 @@
         out_s[2 * p + 1] = total[:, 128:]
         return carry
 
-    spread(0)
+    chunk(0)
     give(0)
-    spread(1)
+    chunk(1)
     give(1)
     keep(0)
     scatter(0)
@@ -460,8 +493,9 @@
     finish(1)
     collect(0)
     collect(1)
-    unfold(0)
-    unfold(1)
+    for m in range(g.chunks):
+        for k in range(g.k):
+            swap(m, k).wait()
     store_out.wait()
 
 
@@ -479,7 +513,7 @@
         functools.partial(kernel, g),
         out_shape=(
             jax.ShapeDtypeStruct(field, BF16),
-            jax.ShapeDtypeStruct((g.mix, channels), F32),
+            jax.ShapeDtypeStruct((g.mix, channels), BF16),
         ),
         in_specs=[anywhere, anywhere, anywhere, vmem, vmem, vmem],
         out_specs=(anywhere, vmem),
@@ -492,6 +526,7 @@
             pltpu.VMEM((256, nlat), F32),
             pltpu.VMEM((kernels, g.near * 32, 128), F32),
             pltpu.VMEM((g.pairs, g.deep, kernels * 256), BF16),
+            pltpu.VMEM((g.pairs, channels, kernels * 256), F32),
             pltpu.VMEM((g.pairs, g.mix, 256), BF16),
             pltpu.VMEM((8 * rows, channels), BF16),
             pltpu.VMEM((8 * rows, channels), BF16),
@@ -505,13 +540,12 @@
             pltpu.VMEM((chunks, g.team, g.piece, 128), BF16),
             pltpu.VMEM((chunks, g.far, g.piece, 128), F32),
             pltpu.VMEM((chunks, g.piece, 128), BF16),
-            pltpu.VMEM((chunks, 2, g.half, 128), BF16),
             pltpu.VMEM(field, BF16),
-            dma((4,)),
+            dma((4 + chunks,)),
             dma((8,)),
             dma((8,)),
-            dma((2 * chunks,)),
-            dma((2 * chunks,)),
+            dma((chunks * (1 + kernels),)),
+            dma((chunks * (1 + kernels),)),
             dma((chunks * g.team,)),
             dma((chunks * g.team,)),
             dma((chunks * g.far,)),
@@ -530,7 +564,8 @@
         row_offset,
         reach,
     )
-    return out.transpose(1, 0, 2), total.reshape(kernels, channels, channels)
+    weight_grad = total.reshape(kernels, channels, channels).astype(F32)
+    return out.transpose(1, 0, 2), weight_grad / jnp.sqrt(jnp.float32(nlat * cols * lon))
 
 
 def solution(mesh):

time: 57.4 us -> 53 us (0.923)
  Pallas kernels: 52.9 us -> 48.5 us
  local copies, waits for them, and re-layouts: 3.7 us -> 1.02 us
  other arithmetic: 0 us -> 2.63 us
    pallas_call x1, Pallas kernels: 52.9 us -> 48.5 us  [on_device(): pl.pallas_call(functools.partial(kernel, g), out_shape=(jax.ShapeDtypeStr...]
    unnamed x4 -> x3, local copies, waits for them, and re-layouts: 3.7 us -> 1.02 us
    div x0 -> x1, other arithmetic: none -> 2.63 us  [on_device(): weight_grad / jnp.sqrt(jnp.float32(nlat * cols * lon))]
where the time goes in v3:
time: 53 us; the launch traced here: 52.8 us
  Pallas kernels  48.5 us (92%)
  other arithmetic  2.63 us (5%)
  local copies, waits for them, and re-layouts  1.02 us (2%)
  between operations  0.65 us (1%)
    pallas_call x1, Pallas kernels, on_device(): pl.pallas_call(functools.partial(kernel, g), out_shape=(jax.ShapeDtypeStr...  48.5 us
    div x1, other arithmetic, on_device(): weight_grad / jnp.sqrt(jnp.float32(nlat * cols * lon))  2.63 us

profile of v3, /device:TPU:1, one launch (start us, length us, event | category | flops | bytes accessed | tf_op | source)
XLA Modules:
  0.0 52.8 jit_solution(11705249675665323850)
XLA Ops:
  0.6 48.5 %shard_map.77 = (bf16[12,384,128]{2,1,0:T(8,128)(2,1)}, bf16[1152,384]{1,0:T(8,128)(2,1)}) custom-call(bf16[12,384,128]{2,1,0:T(8,128)(2,1)} %bitcast.7, bf16[12,384,128]{2,1,0:T(8,128)(2,1)} %bitcast.8, bf16[1152,384]{1,0:T(8,128)(2,1)} %bitcast.10, bf16[3,17,4,384]{3,2,1,0:T(4,128)(2,1)} %bitcast.11, s32[384]{0:T(512)} %ro.1, s32[384]{0:T(512)} %reach.1), custom_call_target="tpu_custom_call" | custom-call | tf_op jit(solution)/shard_map/pallas_call | solution.py:512
  49.2 0.0 copy-start
  49.2 2.6 %convert_multiply_fusion = f32[1152,384]{1,0:T(8,128)} fusion(bf16[1152,384]{1,0:T(8,128)(2,1)} %get-tuple-element.5), kind=kLoop, calls=%fused_computation | loop fusion | flops 884736 | bytes 2654208 | tf_op jit(solution)/shard_map/div | solution.py:568
  51.8 0.0 copy-done
  51.8 1.0 %copy.9 = bf16[384,12,128]{2,0,1:T(8,128)(2,1)} copy(bf16[384,12,128]{2,0,1:T(8,128)(2,1)S(1)} %bitcast.9) | data formatting | bytes 2359296
Async XLA Ops:
  49.2 2.6 %copy-start = (bf16[12,384,128]{2,1,0:T(8,128)(2,1)S(1)}, bf16[12,384,128]{2,1,0:T(8,128)(2,1)}, u32[]{:S(2)}) copy-start(bf16[12,384,128]{2,1,0:T(8,128)(2,1)} %get-tuple-element.4) | copy-start | bytes 3538948

commit v4 on v3

--- a/solution.py
+++ b/solution.py
@@ -91,7 +91,6 @@
     team_in,
     far_in,
     final,
-    out_s,
     local_sem,
     halo_send,
     halo_recv,
@@ -422,7 +421,7 @@
 
     def lay_own(m):
         there = landing(m, owned(me, m)[0])
-        return pltpu.make_async_copy(final.at[m], there, local_sem.at[4 + m])
+        return pltpu.make_async_copy(final.at[m], there, local_sem.at[3 + m])
 
     def finish(m):
         n, mine = owned(me, m)
@@ -472,8 +471,8 @@
 
     def inward(p, carry):
         total = jnp.dot(wt[...], sp[p], preferred_element_type=F32).astype(BF16)
-        out_s[2 * p] = total[:, :128]
-        out_s[2 * p + 1] = total[:, 128:]
+        out[2 * p] = total[:, :128]
+        out[2 * p + 1] = total[:, 128:]
         return carry
 
     chunk(0)
@@ -485,8 +484,6 @@
     keep(1)
     scatter(1)
     lax.fori_loop(0, g.pairs, inward, 0)
-    store_out = pltpu.make_async_copy(out_s, out, local_sem.at[3])
-    store_out.start()
     add(0)
     add(1)
     finish(0)
@@ -496,7 +493,6 @@
     for m in range(g.chunks):
         for k in range(g.k):
             swap(m, k).wait()
-    store_out.wait()
 
 
 def on_device(cotangent, layer_input, filter_values, weights, row_offset, reach):
@@ -512,11 +508,11 @@
     out, total = pl.pallas_call(
         functools.partial(kernel, g),
         out_shape=(
-            jax.ShapeDtypeStruct(field, BF16),
-            jax.ShapeDtypeStruct((g.mix, channels), BF16),
+            pltpu.VMEM(field, BF16),
+            pltpu.VMEM((g.mix, channels), BF16),
         ),
         in_specs=[anywhere, anywhere, anywhere, vmem, vmem, vmem],
-        out_specs=(anywhere, vmem),
+        out_specs=(vmem, vmem),
         scratch_shapes=[
             pltpu.VMEM((g.tall, channels, cols), BF16),
             pltpu.VMEM(field, BF16),
@@ -540,8 +536,7 @@
             pltpu.VMEM((chunks, g.team, g.piece, 128), BF16),
             pltpu.VMEM((chunks, g.far, g.piece, 128), F32),
             pltpu.VMEM((chunks, g.piece, 128), BF16),
-            pltpu.VMEM(field, BF16),
-            dma((4 + chunks,)),
+            dma((3 + chunks,)),
             dma((8,)),
             dma((8,)),
             dma((chunks * (1 + kernels),)),

time: 53 us -> 50.7 us (0.957)
  other arithmetic: 2.63 us -> 1.36 us
  Pallas kernels: 48.5 us -> 47.5 us
    div x1, other arithmetic: 2.63 us -> 1.36 us  [on_device(): weight_grad / jnp.sqrt(jnp.float32(nlat * cols * lon))]
    pallas_call x1, Pallas kernels: 48.5 us -> 47.5 us  [on_device(): pl.pallas_call(functools.partial(kernel, g), out_shape=(pltpu.VMEM(field,...]
where the time goes in v4:
time: 50.7 us; the launch traced here: 50.6 us
  Pallas kernels  47.5 us (94%)
  other arithmetic  1.36 us (3%)
  local copies, waits for them, and re-layouts  1.02 us (2%)
  between operations  0.64 us (1%)
    pallas_call x1, Pallas kernels, on_device(): pl.pallas_call(functools.partial(kernel, g), out_shape=(pltpu.VMEM(field,...  47.5 us
    div x1, other arithmetic, on_device(): weight_grad / jnp.sqrt(jnp.float32(nlat * cols * lon))  1.36 us
    unnamed x1, local copies, waits for them, and re-layouts  1.02 us

profile of v4, /device:TPU:1, one launch (start us, length us, event | category | flops | bytes accessed | tf_op | source)
XLA Modules:
  0.0 50.6 jit_solution(18224814621392367933)
XLA Ops:
  0.6 47.5 %shard_map.77 = (bf16[12,384,128]{2,1,0:T(8,128)(2,1)S(1)}, bf16[1152,384]{1,0:T(8,128)(2,1)S(1)}) custom-call(bf16[12,384,128]{2,1,0:T(8,128)(2,1)} %bitcast.8, bf16[12,384,128]{2,1,0:T(8,128)(2,1)} %bitcast.9, bf16[1152,384]{1,0:T(8,128)(2,1)} %bitcast.10, bf16[3,17,4,384]{3,2,1,0:T(4,128)(2,1)} %bitcast.11, s32[384]{0:T(512)} %ro.1, s32[384]{0:T(512)} %reach.1), custom_call_target="tpu_custom_call" | custom-call | tf_op jit(solution)/shard_map/pallas_call | solution.py:508
  48.2 1.0 %copy.9 = bf16[384,12,128]{2,0,1:T(8,128)(2,1)} copy(bf16[384,12,128]{2,0,1:T(8,128)(2,1)S(1)} %bitcast.6) | data formatting | bytes 2359296
  49.2 1.4 %convert_multiply_fusion = f32[1152,384]{1,0:T(8,128)} fusion(bf16[1152,384]{1,0:T(8,128)(2,1)S(1)} %get-tuple-element.5), kind=kLoop, calls=%fused_computation | loop fusion | flops 884736 | bytes 2654208 | tf_op jit(solution)/shard_map/div | solution.py:563

commit v5 on v4

--- a/solution.py
+++ b/solution.py
@@ -1,4 +1,5 @@
 import functools
+import math
 
 import jax
 import jax.numpy as jnp
@@ -64,11 +65,14 @@
     cot,
     xin,
     w_in,
+    fv_in,
+    ro_in,
+    reach_in,
+    out,
+    total_out,
     fv,
     ro,
     reach,
-    out,
-    total_out,
     cot_s,
     x_s,
     xt,
@@ -145,7 +149,13 @@
     load_cot = pltpu.make_async_copy(cot, cot_s.at[pl.ds(g.rim, g.rows)], local_sem.at[0])
     load_x = pltpu.make_async_copy(xin, x_s, local_sem.at[1])
     load_w = pltpu.make_async_copy(w_in, w_s, local_sem.at[2])
+    load_taps = [
+        pltpu.make_async_copy(source, target, local_sem.at[3 + g.chunks + n])
+        for n, (source, target) in enumerate(((fv_in, fv), (ro_in, ro), (reach_in, reach)))
+    ]
     load_cot.start()
+    for copy in load_taps:
+        copy.start()
     load_x.start()
     load_w.start()
     load_cot.wait()
@@ -182,6 +192,8 @@
     for copy in sends:
         copy.start()
 
+    for copy in load_taps:
+        copy.wait()
     entries = g.k * g.taps * g.span
     for k in range(g.k):
         for t in range(g.taps):
@@ -495,6 +507,18 @@
             swap(m, k).wait()
 
 
+def deliver(scale, field, total, out, weight_grad, wide, sems):
+    store = [pltpu.make_async_copy(field, out, sems.at[0])]
+    store[0].start()
+    kernels, channels, _ = wide.shape
+    for k in range(kernels):
+        wide[k] = total[k * channels : (k + 1) * channels, :].astype(F32) * scale
+        store.append(pltpu.make_async_copy(wide.at[k], weight_grad.at[k], sems.at[1 + k]))
+        store[-1].start()
+    for copy in store:
+        copy.wait()
+
+
 def on_device(cotangent, layer_input, filter_values, weights, row_offset, reach):
     channels, rows, cols = cotangent.shape
     kernels, nlat, span, taps = filter_values.shape
@@ -511,9 +535,12 @@
             pltpu.VMEM(field, BF16),
             pltpu.VMEM((g.mix, channels), BF16),
         ),
-        in_specs=[anywhere, anywhere, anywhere, vmem, vmem, vmem],
+        in_specs=[anywhere] * 6,
         out_specs=(vmem, vmem),
         scratch_shapes=[
+            pltpu.VMEM((kernels, taps, span, nlat), BF16),
+            pltpu.VMEM((nlat,), jnp.int32),
+            pltpu.VMEM((nlat,), jnp.int32),
             pltpu.VMEM((g.tall, channels, cols), BF16),
             pltpu.VMEM(field, BF16),
             pltpu.VMEM((rows * cols, channels), BF16),
@@ -536,7 +563,7 @@
             pltpu.VMEM((chunks, g.team, g.piece, 128), BF16),
             pltpu.VMEM((chunks, g.far, g.piece, 128), F32),
             pltpu.VMEM((chunks, g.piece, 128), BF16),
-            dma((3 + chunks,)),
+            dma((6 + chunks,)),
             dma((8,)),
             dma((8,)),
             dma((chunks * (1 + kernels),)),
@@ -559,8 +586,16 @@
         row_offset,
         reach,
     )
-    weight_grad = total.reshape(kernels, channels, channels).astype(F32)
-    return out.transpose(1, 0, 2), weight_grad / jnp.sqrt(jnp.float32(nlat * cols * lon))
+    shape = (kernels, channels, channels)
+    input_grad, weight_grad = pl.pallas_call(
+        functools.partial(deliver, 1.0 / math.sqrt(nlat * cols * lon)),
+        out_shape=(jax.ShapeDtypeStruct(field, BF16), jax.ShapeDtypeStruct(shape, F32)),
+        in_specs=[vmem, vmem],
+        out_specs=(anywhere, anywhere),
+        scratch_shapes=[pltpu.VMEM(shape, F32), dma((1 + kernels,))],
+        compiler_params=pltpu.CompilerParams(vmem_limit_bytes=16 * 2**20),
+    )(out, total)
+    return input_grad.transpose(1, 0, 2), weight_grad
 
 
 def solution(mesh):

time: 50.7 us -> 49.6 us (0.978)
  Pallas kernels: 47.5 us -> 48.9 us
  other arithmetic: 1.36 us -> 0 us
  local copies, waits for them, and re-layouts: 1.02 us -> 0 us
    pallas_call x0 -> x1, Pallas kernels: none -> 1.63 us  [on_device(): pl.pallas_call(functools.partial(deliver, 1.0 / math.sqrt(nlat * cols * l...]
    div x1 -> x0, other arithmetic: 1.36 us -> none  [on_device(): weight_grad / jnp.sqrt(jnp.float32(nlat * cols * lon))]
    unnamed x1 -> x0, local copies, waits for them, and re-layouts: 1.02 us -> none
where the time goes in v5:
time: 49.6 us; the launch traced here: 49.5 us
  Pallas kernels  48.9 us (99%)
  between operations  0.64 us (1%)
    pallas_call x1, Pallas kernels, on_device(): pl.pallas_call(functools.partial(kernel, g), out_shape=(pltpu.VMEM(field,...  47.3 us
    pallas_call x1, Pallas kernels, on_device(): pl.pallas_call(functools.partial(deliver, 1.0 / math.sqrt(nlat * cols * l...  1.63 us

profile of v5, /device:TPU:1, one launch (start us, length us, event | category | flops | bytes accessed | tf_op | source)
XLA Modules:
  0.0 49.5 jit_solution(13448953330770146587)
XLA Ops:
  0.6 47.3 %shard_map.77 = (bf16[12,384,128]{2,1,0:T(8,128)(2,1)S(1)}, bf16[1152,384]{1,0:T(8,128)(2,1)S(1)}) custom-call(bf16[12,384,128]{2,1,0:T(8,128)(2,1)} %bitcast.5, bf16[12,384,128]{2,1,0:T(8,128)(2,1)} %bitcast.6, bf16[1152,384]{1,0:T(8,128)(2,1)} %bitcast.7, bf16[3,17,4,384]{3,2,1,0:T(4,128)(2,1)} %bitcast.8, s32[384]{0:T(512)} %ro_in.1, s32[384]{0:T(512)} %reach_in.1), custom_call_target="tpu_custom_call" | custom-call | tf_op jit(solution)/shard_map/pallas_call | solution.py:532
  47.9 1.6 %shard_map.78 = (bf16[12,384,128]{2,1,0:T(8,128)(2,1)}, f32[3,384,384]{2,1,0:T(8,128)}) custom-call(bf16[12,384,128]{2,1,0:T(8,128)(2,1)S(1)} %get-tuple-element.6.field, bf16[1152,384]{1,0:T(8,128)(2,1)S(1)} %get-tuple-element.7.total), custom_call_target="tpu_custom_call" | custom-call | tf_op jit(solution)/shard_map/pallas_call | solution.py:590

commit v6 on v5

--- a/solution.py
+++ b/solution.py
@@ -411,13 +411,6 @@
             for d in range(1, g.far):
                 to_far(m, d).start()
 
-        for d in range(1, g.team):
-            valid, copy = to_owner(m, d)
-
-            @pl.when(valid)
-            def _():
-                copy.wait_send()
-
     def landing(m, n):
         b, r = n // (g.tier // g.piece), lax.rem(n, g.tier // g.piece)
         k, r = r // (g.slim // g.piece), lax.rem(r, g.slim // g.piece)
@@ -476,7 +469,15 @@
         for k in range(g.k):
             swap(m, k).start()
 
-        @pl.when(mine)
+    def drain(m):
+        for d in range(1, g.team):
+            valid, copy = to_owner(m, d)
+
+            @pl.when(valid)
+            def _():
+                copy.wait_send()
+
+        @pl.when(owned(me, m)[1])
         def _():
             for d in range(1, g.team):
                 from_owner(m, d).wait_send()
@@ -502,6 +503,8 @@
     finish(1)
     collect(0)
     collect(1)
+    for m in range(g.chunks):
+        drain(m)
     for m in range(g.chunks):
         for k in range(g.k):
             swap(m, k).wait()

time: 49.6 us -> 49.6 us (level)
  no operation moved by 1% of the time
where the time goes in v6:
time: 49.6 us; the launch traced here: 49.5 us
  Pallas kernels  48.9 us (99%)
  between operations  0.64 us (1%)
    pallas_call x1, Pallas kernels, on_device(): pl.pallas_call(functools.partial(kernel, g), out_shape=(pltpu.VMEM(field,...  47.3 us
    pallas_call x1, Pallas kernels, on_device(): pl.pallas_call(functools.partial(deliver, 1.0 / math.sqrt(nlat * cols * l...  1.63 us

profile of v6, /device:TPU:1, one launch (start us, length us, event | category | flops | bytes accessed | tf_op | source)
XLA Modules:
  0.0 49.5 jit_solution(10969030138980681963)
XLA Ops:
  0.6 47.3 %shard_map.77 = (bf16[12,384,128]{2,1,0:T(8,128)(2,1)S(1)}, bf16[1152,384]{1,0:T(8,128)(2,1)S(1)}) custom-call(bf16[12,384,128]{2,1,0:T(8,128)(2,1)} %bitcast.5, bf16[12,384,128]{2,1,0:T(8,128)(2,1)} %bitcast.6, bf16[1152,384]{1,0:T(8,128)(2,1)} %bitcast.7, bf16[3,17,4,384]{3,2,1,0:T(4,128)(2,1)} %bitcast.8, s32[384]{0:T(512)} %ro_in.1, s32[384]{0:T(512)} %reach_in.1), custom_call_target="tpu_custom_call" | custom-call | tf_op jit(solution)/shard_map/pallas_call | solution.py:535
  47.9 1.6 %shard_map.78 = (bf16[12,384,128]{2,1,0:T(8,128)(2,1)}, f32[3,384,384]{2,1,0:T(8,128)}) custom-call(bf16[12,384,128]{2,1,0:T(8,128)(2,1)S(1)} %get-tuple-element.6.field, bf16[1152,384]{1,0:T(8,128)(2,1)S(1)} %get-tuple-element.7.total), custom_call_target="tpu_custom_call" | custom-call | tf_op jit(solution)/shard_map/pallas_call | solution.py:593

commit v7 on v6

--- a/solution.py
+++ b/solution.py
@@ -287,11 +287,8 @@
         inner[p] = jnp.dot(wide, deep, preferred_element_type=F32)
 
     load_x.wait()
-    load_w.wait()
     for i in range(rows):
         xt[i * 128 : (i + 1) * 128, :] = x_s[i].T
-    for k in range(g.k):
-        wt[:, k * g.c : (k + 1) * g.c] = w_s[k * g.c : (k + 1) * g.c, :].T
 
     def lay_rim(w):
         at = 16 * ((w + 1) // 2)
@@ -496,6 +493,9 @@
     scatter(0)
     keep(1)
     scatter(1)
+    load_w.wait()
+    for k in range(g.k):
+        wt[:, k * g.c : (k + 1) * g.c] = w_s[k * g.c : (k + 1) * g.c, :].T
     lax.fori_loop(0, g.pairs, inward, 0)
     add(0)
     add(1)

time: 49.6 us -> 49.3 us (level)
  no operation moved by 1% of the time
where the time goes in v7:
time: 49.3 us
  Pallas kernels  48.6 us (99%)
  between operations  0.64 us (1%)
    pallas_call x1, Pallas kernels, on_device(): pl.pallas_call(functools.partial(kernel, g), out_shape=(pltpu.VMEM(field,...  47 us
    pallas_call x1, Pallas kernels, on_device(): pl.pallas_call(functools.partial(deliver, 1.0 / math.sqrt(nlat * cols * l...  1.63 us

profile of v7, /device:TPU:1, one launch (start us, length us, event | category | flops | bytes accessed | tf_op | source)
XLA Modules:
  0.0 49.3 jit_solution(17145828785904830013)
XLA Ops:
  0.6 47.0 %shard_map.77 = (bf16[12,384,128]{2,1,0:T(8,128)(2,1)S(1)}, bf16[1152,384]{1,0:T(8,128)(2,1)S(1)}) custom-call(bf16[12,384,128]{2,1,0:T(8,128)(2,1)} %bitcast.5, bf16[12,384,128]{2,1,0:T(8,128)(2,1)} %bitcast.6, bf16[1152,384]{1,0:T(8,128)(2,1)} %bitcast.7, bf16[3,17,4,384]{3,2,1,0:T(4,128)(2,1)} %bitcast.8, s32[384]{0:T(512)} %ro_in.1, s32[384]{0:T(512)} %reach_in.1), custom_call_target="tpu_custom_call" | custom-call | tf_op jit(solution)/shard_map/pallas_call | solution.py:535
  47.6 1.6 %shard_map.78 = (bf16[12,384,128]{2,1,0:T(8,128)(2,1)}, f32[3,384,384]{2,1,0:T(8,128)}) custom-call(bf16[12,384,128]{2,1,0:T(8,128)(2,1)S(1)} %get-tuple-element.6.field, bf16[1152,384]{1,0:T(8,128)(2,1)S(1)} %get-tuple-element.7.total), custom_call_target="tpu_custom_call" | custom-call | tf_op jit(solution)/shard_map/pallas_call | solution.py:593
